TPU v7x, 128 devices: a whole 4x4x4 slice. The times are simulated.
128 devices in a mesh: dp: 8 (over y, x_hi), expert: 16 (over z, x_lo, core).
Axes of the slice: x: 4 (x_hi: 2, x_lo: 2; x = x_hi * 2 + x_lo), y: 4, z: 4, core: 2. Of those that a mesh axis runs over, the one named last changes fastest.
Arguments:
- tokens: bfloat16 [4096, 2048], P('expert'), may hold values from -6 to 6
- out_grad: bfloat16 [4096, 2048], P('expert'), may hold values from -2 to 2
- expert_ids: int32 [4096, 2], P('expert'), may hold values from 0 to 15, all different within a row; in each aligned block of 256 rows (0 to 255, 256 to 511, ...) at most 64 rows name the same one
- gate_probs: bfloat16 [4096, 2], P('expert'), may hold values from 0.099609375 to 1
- w_gate: bfloat16 [16, 768, 2048], P('expert', 'dp'), may hold values from -0.125 to 0.125
- w_up: bfloat16 [16, 768, 2048], P('expert', 'dp'), may hold values from -0.125 to 0.125
- w_down: bfloat16 [16, 768, 2048], P('expert', 'dp'), may hold values from -0.21875 to 0.21875
Outputs:
- token_grad: float32 [4096, 2048], P('expert', 'dp')
- prob_grad: float32 [4096, 2], P('expert')
- grad_gate: float32 [16, 768, 2048], P('expert', 'dp')
- grad_up: float32 [16, 768, 2048], P('expert', 'dp')
- grad_down: float32 [16, 768, 2048], P('expert', 'dp')
Inputs may be any that keep to these rules, and one draw needn't show every extreme that they name: `expert_ids`: in the rows of one device no expert is named by more than 64 rows; the 2 experts of a token differ.
All inputs are finite; a program needn't handle non-finite values.
Results may differ from a plain program's by a relative error of at most 0.02.
Values may be sent and summed in bfloat16 or wider, within the bound.
A program may use at most 128 MiB of HBM per device.

v0:
```python
import jax
import jax.numpy as jnp
from jax import lax
from jax.sharding import PartitionSpec as P


def slot_tables(expert_ids, experts, capacity):
    tokens, routes = expert_ids.shape
    flattened = expert_ids.reshape(-1)
    one_hot = (flattened[:, None] == jnp.arange(experts, dtype=jnp.int32)[None, :]).astype(
        jnp.int32
    )
    earlier = jnp.cumsum(one_hot, axis=0) - one_hot
    position = jnp.sum(earlier * one_hot, axis=1)
    target = flattened * capacity + position
    serial = jnp.arange(tokens * routes, dtype=jnp.int32)
    slot_index = (
        jnp.zeros((experts * capacity,), jnp.int32)
        .at[target]
        .set(serial)
        .reshape(experts, capacity)
    )
    filled = (
        jnp.zeros((experts * capacity,), jnp.float32).at[target].set(1.0).reshape(experts, capacity)
    )
    return (slot_index, filled)


def expert_math(slot_x, slot_dy, slot_p, weight_gate, weight_up, weight_down):
    weight_form = "efd"

    def inward(values, weight):
        return jnp.einsum(
            "ecd," + weight_form + "->ecf", values, weight, preferred_element_type=jnp.float32
        )

    def outward(values, weight):
        return jnp.einsum(
            "ecf," + weight_form + "->ecd", values, weight, preferred_element_type=jnp.float32
        )

    gate_pre = inward(slot_x, weight_gate)
    up_pre = inward(slot_x, weight_up)
    sigmoid_gate = jax.nn.sigmoid(gate_pre)
    active = gate_pre * sigmoid_gate
    hidden = active * up_pre
    hidden_low = hidden.astype(jnp.bfloat16)
    backed = inward(slot_dy, weight_down)
    prob_slot = jnp.sum(hidden * backed, axis=-1)
    prob_column = slot_p.astype(jnp.float32)[..., None]
    grad_hidden = prob_column * backed
    grad_gate_pre = (
        grad_hidden * up_pre * sigmoid_gate * (1.0 + gate_pre * (1.0 - sigmoid_gate))
    ).astype(jnp.bfloat16)
    grad_up_pre = (grad_hidden * active).astype(jnp.bfloat16)
    scaled = (prob_column * slot_dy.astype(jnp.float32)).astype(jnp.bfloat16)
    dx_slot = outward(grad_gate_pre, weight_gate) + outward(grad_up_pre, weight_up)
    partial_gate = jnp.einsum(
        "ecf,ecd->efd", grad_gate_pre, slot_x, preferred_element_type=jnp.float32
    )
    partial_up = jnp.einsum("ecf,ecd->efd", grad_up_pre, slot_x, preferred_element_type=jnp.float32)
    partial_down = jnp.einsum(
        "ecf,ecd->efd", hidden_low, scaled, preferred_element_type=jnp.float32
    )
    return (dx_slot, prob_slot, (partial_gate, partial_up, partial_down))


def on_device(tokens, out_grad, expert_ids, gate_probs, w_gate, w_up, w_down):
    experts = lax.axis_size("expert")
    rows_here, top_count = expert_ids.shape
    capacity = 2 * rows_here * top_count // experts
    width = tokens.shape[1]
    slot_index, filled = slot_tables(expert_ids, experts, capacity)
    token_row = slot_index // top_count
    slot_x = tokens[token_row]
    slot_dy = out_grad[token_row]
    slot_p = gate_probs.reshape(-1)[slot_index] * filled.astype(jnp.bfloat16)
    local_ff = w_gate.shape[1]
    dx_sum = jnp.zeros((rows_here, width), jnp.float32)
    prob_sum = jnp.zeros((rows_here * top_count,), jnp.float32)
    grads = jnp.zeros((experts, 3, local_ff, width), jnp.bfloat16)
    part_gate = lax.all_gather(w_gate, "expert", axis=0, tiled=True)
    part_up = lax.all_gather(w_up, "expert", axis=0, tiled=True)
    part_down = lax.all_gather(w_down, "expert", axis=0, tiled=True)
    dx_slot, prob_slot, partials = expert_math(
        slot_x, slot_dy, slot_p, part_gate, part_up, part_down
    )
    dx_sum = dx_sum.at[(slot_index // top_count).reshape(-1)].add(
        (dx_slot * filled[..., None]).reshape(-1, width)
    )
    prob_sum = prob_sum.at[slot_index.reshape(-1)].add((prob_slot * filled).reshape(-1))
    stacked = jnp.stack(partials, axis=1).astype(jnp.bfloat16)
    grads = lax.dynamic_update_slice_in_dim(grads, stacked, jnp.int32(0), 0)
    dx_sum, prob_sum, grads = (dx_sum, prob_sum, grads)
    token_grad = lax.psum_scatter(
        dx_sum.astype(jnp.bfloat16), "dp", scatter_dimension=1, tiled=True
    ).astype(jnp.float32)
    prob_grad = lax.psum(prob_sum.reshape(rows_here, top_count), "dp")
    returned = lax.psum_scatter(
        lax.optimization_barrier(grads).astype(jnp.float32).astype(jnp.bfloat16),
        "expert",
        scatter_dimension=0,
        tiled=True,
    ).astype(jnp.float32)
    grad_gate = returned[:, 0]
    grad_up = returned[:, 1]
    grad_down = returned[:, 2]
    return (token_grad, prob_grad, grad_gate, grad_up, grad_down)


def solution(mesh):
    in_specs = (
        P("expert", None),
        P("expert", None),
        P("expert", None),
        P("expert", None),
        P("expert", "dp", None),
        P("expert", "dp", None),
        P("expert", "dp", None),
    )
    out_specs = (
        P("expert", "dp"),
        P("expert", None),
        P("expert", "dp", None),
        P("expert", "dp", None),
        P("expert", "dp", None),
    )
    return jax.shard_map(
        on_device, mesh=mesh, in_specs=in_specs, out_specs=out_specs, check_vma=False
    )
```

profile of v0, /device:TPU:1, one launch (start us, length us, event | category | flops | bytes accessed | tf_op | source)
XLA Modules:
  0.0 668.3 jit_solution(16618328737865911497)
XLA Ops:
  13.1 2.4 scatter_custom_fusion
  16.7 6.8 %gather_fusion = bf16[1024]{0:T(1024)(128)(2,1)S(1)} fusion(bf16[512]{0:T(512)(128)(2,1)S(1)} %reshape.186, s32[1024]{0:T(1024)S(1)} %broadcast_clamp_fusion.1), kind=kCustom, calls=%fused_computation | custom fusion | bytes 8192 | tf_op jit(solution)/shard_map/gather | solution.py:77
  23.6 2.6 scatter_custom_fusion.1
  26.3 6.1 gather_fusion.2
  32.4 6.0 gather_fusion.1
  38.4 17.4 %all-gather.6.cloned.1.call-done = bf16[16,96,2048]{2,1,0:T(8,128)(2,1)} async-done(((bf16[1,96,2048]{2,1,0:T(8,128)(2,1)}), bf16[16,96,2048]{2,1,0:T(8,128)(2,1)}) %all-gather.6.cloned.1.call-update) | async-done | bytes 6291472 | tf_op jit(solution)/shard_map/all_gather | solution.py:83
  55.8 6.5 fusion.21
  62.3 38.5 %all-gather.8.cloned.1.call-done = bf16[16,96,2048]{2,1,0:T(8,128)(2,1)} async-done(((bf16[1,96,2048]{2,1,0:T(8,128)(2,1)}), bf16[16,96,2048]{2,1,0:T(8,128)(2,1)}) %all-gather.8.cloned.1.call-update) | async-done | bytes 6291472 | tf_op jit(solution)/shard_map/all_gather | solution.py:82
  100.8 6.5 fusion.22
  107.3 38.5 %all-gather.4.cloned.1.call-done = bf16[16,96,2048]{2,1,0:T(8,128)(2,1)} async-done(((bf16[1,96,2048]{2,1,0:T(8,128)(2,1)}), bf16[16,96,2048]{2,1,0:T(8,128)(2,1)}) %all-gather.4.cloned.1.call-update) | async-done | bytes 6291472 | tf_op jit(solution)/shard_map/all_gather | solution.py:84
  145.8 6.8 %multiply_reduce_fusion = (f32[16,64]{1,0:T(8,128)S(1)}, bf16[16,64,96]{2,1,0:T(8,128)(2,1)S(1)}, bf16[16,64,96]{2,1,0:T(8,128)(2,1)S(1)}) fusion(f32[16,64,96]{2,1,0:T(8,128)S(1)} %fusion.21, f32[16,64,96]{2,1,0:T(8,128)S(1)} %fusion.22, f32[16,64]{1,0:T(8,128)S(1)} %multiply_convert_fusion.4, bf16[16,64,2048]{2,1,0:T(8,128)(2,1)} %bitcast.71, ...), kind=kOutput, calls=%fused_computation.20 | convolution fusion | flops 404323328 | bytes 11673600 | tf_op jit(solution)/shard_map/ecd,efd->ecf/dot_general | solution.py:33
  152.6 4.5 convert_bitcast_fusion.1
  158.7 4.5 add_multiply_fusion
  163.2 15.4 %scatter_custom_fusion.2 = f32[256,2048]{1,0:T(8,128)S(1)} fusion(s32[1024]{0:T(1024)S(1)} %get-tuple-element.24, f32[1024,2048]{1,0:T(8,128)} %bitcast.73, f32[]{:T(128)} %constant.13.clone.1), kind=kCustom, calls=%fused_computation.15 | custom fusion | flops 2097152 | bytes 2097664 | tf_op jit(solution)/shard_map/scatter-add | solution.py:88
  179.8 4.2 convert_bitcast_fusion.2
  184.0 1.9 convert_bitcast_fusion
  185.9 12.6 %pad_maximum_fusion = bf16[16,3,96,2048]{3,2,0,1:T(8,128)(2,1)} fusion(bf16[16,1,96,2048]{3,2,0,1:T(8,128)(2,1)S(1)} %convert_bitcast_fusion, bf16[16,1,96,2048]{3,2,0,1:T(8,128)(2,1)S(1)} %bitcast.68, bf16[16,1,96,2048]{3,2,0,1:T(8,128)(2,1)S(1)} %convert_bitcast_fusion.2), kind=kLoop, calls=%fused_computation.7 | loop fusion | flops 18874368 | bytes 37748736 | tf_op jit(solution)/shard_map/stack | solution.py:92
  199.8 7.6 %scatter_custom_fusion.3 = f32[512]{0:T(512)S(1)} fusion(s32[1024]{0:T(1024)S(1)} %get-tuple-element.23, f32[1024]{0:T(1024)S(1)} %mul.95, f32[]{:T(128)} %constant.13.clone.1), kind=kCustom, calls=%fused_computation.62 | custom fusion | flops 1024 | bytes 2052 | tf_op jit(solution)/shard_map/scatter-add | solution.py:91
  207.6 36.5 %psum.7 = f32[256,2]{1,0:T(8,128)S(1)} all-reduce(f32[256,2]{1,0:T(8,128)S(1)} %reshape.190), channel_id=1, replica_groups=mesh['dp'=8,'expert'=16] {'dp'}, use_global_device_ids=true, to_apply=%region_9.10 | all-reduce | flops 512 | bytes 4096 | tf_op jit(solution)/shard_map/psum | solution.py:98
  244.8 5.6 reduce-scatter.5.cloned.1.call-done
  250.3 1.6 convert_element_type.55
  252.0 406.1 %all-reduce.3.cloned.1.call-done = bf16[16,3,96,2048]{3,2,0,1:T(8,128)(2,1)} async-done(((bf16[16,3,96,2048]{3,2,0,1:T(8,128)(2,1)}), bf16[16,3,96,2048]{3,2,0,1:T(8,128)(2,1)}) %all-reduce.3.cloned.1.call-update) | async-done | bytes 18874384
  658.1 2.2 dynamic-slice_convert_fusion
  660.3 1.5 slice_bitcast_fusion
  (71 shorter events, 12.0 us)
Async XLA Ops:
  7.2 19.2 %copy-start = (bf16[256,2048]{1,0:T(8,128)(2,1)S(1)}, bf16[256,2048]{1,0:T(8,128)(2,1)}, u32[]{:S(2)}) copy-start(bf16[256,2048]{1,0:T(8,128)(2,1)} %param.7) | copy-start | bytes 3145732
  7.2 48.6 %all-gather.6.cloned.1.call-start = ((), (), s32[]{:S(2)}) async-start(), calls=%async_computation.2 | async-start | bytes 6684672 | tf_op jit(solution)/shard_map/all_gather | solution.py:83
  7.9 92.9 %all-gather.8.cloned.1.call-start = ((), (), s32[]{:S(2)}) async-start(), calls=%async_computation.3 | async-start | bytes 6684672 | tf_op jit(solution)/shard_map/all_gather | solution.py:82
  8.7 137.1 %all-gather.4.cloned.1.call-start = ((), (), s32[]{:S(2)}) async-start(), calls=%async_computation.1 | async-start | bytes 6684672 | tf_op jit(solution)/shard_map/all_gather | solution.py:84
  9.4 240.9 %reduce-scatter.5.cloned.1.call-start = ((), (), s32[]{:S(2)}) async-start(), calls=%async_computation.4 | async-start | bytes 1179648 | tf_op jit(solution)/shard_map/reduce_scatter | solution.py:95
  26.3 6.1 copy-start.2
  145.8 11.3 %slice-start = ((s8[6291456]{0:T(1024)(128)(4,1)}), s8[4194304]{0:T(1024)(128)(4,1)S(1)}, s32[]{:S(2)}) async-start(s8[6291456]{0:T(1024)(128)(4,1)} %bitcast.65), calls=%async_computation.6 | async-start | bytes 8388608
  145.8 6.8 %copy-start.3 = (bf16[1024,2048]{1,0:T(8,128)(2,1)S(1)}, bf16[1024,2048]{1,0:T(8,128)(2,1)}, u32[]{:S(2)}) copy-start(bf16[1024,2048]{1,0:T(8,128)(2,1)} %gather_fusion.2) | copy-start | bytes 12582916
  145.8 11.3 %slice-start.1 = ((s8[6291456]{0:T(1024)(128)(4,1)}), s8[2097152]{0:T(1024)(128)(4,1)S(1)}, s32[]{:S(2)}) async-start(s8[6291456]{0:T(1024)(128)(4,1)} %bitcast.65), calls=%async_computation.7 | async-start | bytes 4194304
  152.6 5.8 slice-start.4
  157.1 1.6 slice-start.5
  179.8 478.4 %all-reduce.3.cloned.1.call-start = ((), (), s32[]{:S(2)}) async-start(), calls=%async_computation.5 | async-start | bytes 37748736
  179.8 4.2 copy-start.4
  179.8 6.1 slice-start.2
  184.0 1.9 slice-start.3
  198.5 0.7 copy-start.5
  198.6 463.2 %copy-start.1 = (bf16[256,2048]{1,0:T(8,128)(2,1)S(1)}, bf16[256,2048]{1,0:T(8,128)(2,1)}, u32[]{:S(2)}) copy-start(bf16[256,2048]{1,0:T(8,128)(2,1)} %param.7) | copy-start | bytes 3145732
Sparse Core Ops, SparseCore 0:
  9.7 46.0 all-gather.5
  57.5 43.2 all-gather.7
  102.5 43.2 all-gather.3
  179.9 70.4 reduce-scatter.4
  252.9 405.1 all-reduce.2
where the time goes:
time: 669 us; the launch traced here: 668 us
  waiting for transfers between devices  508 us (76%)
  other arithmetic  42.6 us (6%)
  blocking collectives  36.5 us (5%)
  matrix products  35.9 us (5%)
  local copies, waits for them, and re-layouts  30.8 us (5%)
  between operations  14.1 us (2%)
    unnamed x6, waiting for transfers between devices  408 us
    all_gather x1, waiting for transfers between devices, on_device(): part_down = lax.all_gather(w_down, 'expert', axis=0, tiled=True)  38.5 us
    all_gather x1, waiting for transfers between devices, on_device(): part_gate = lax.all_gather(w_gate, 'expert', axis=0, tiled=True)  38.5 us
    psum x1, blocking collectives, on_device(): prob_grad = lax.psum(prob_sum.reshape(rows_here, top_count), 'dp')  36.5 us
    dot_general x3, matrix products, inward(): jnp.einsum('ecd,' + weight_form + '->ecf', values, weight, preferred_elem...  19.7 us
    all_gather x1, waiting for transfers between devices, on_device(): part_up = lax.all_gather(w_up, 'expert', axis=0, tiled=True)  17.4 us
    scatter-add x1, other arithmetic, on_device(): dx_sum.at[(slot_index // top_count).reshape(-1)]  15.4 us
  transfers between devices with their start and end apart: 5, of which 5 were waited for; matrix products, arithmetic and copies ran while one was open for 11% of the time, Pallas kernels for 0%

commit v1 on v0

v1 whole, which is shorter than its diff:
```python
import jax
import jax.numpy as jnp
from jax import lax
from jax.experimental import pallas as pl
from jax.experimental.pallas import tpu as pltpu
from jax.sharding import PartitionSpec as P

MESH = pl.DeviceIdType.MESH
F32 = jnp.float32
BF16 = jnp.bfloat16

D = 2048
FF = 96
TOK = 256
CAP = 64
Q = 512
ROWS = 8 * CAP
HALF = ROWS // 2


def dot(a, b):
    return jnp.dot(a, b, preferred_element_type=F32)


def dot_nt(a, b):
    return lax.dot_general(a, b, (((1,), (1,)), ((), ())), preferred_element_type=F32)


def dot_tn(a, b):
    return lax.dot_general(a, b, (((0,), (0,)), ((), ())), preferred_element_type=F32)


def kernel(
    tok,
    dy,
    meta,
    wg,
    wu,
    wd,
    o_tok,
    o_prob,
    o_g,
    o_u,
    o_d,
    mb,
    xo,
    raw,
    stage,
    slots,
    wgu,
    wdn,
    upper,
    p_own,
    p_oth,
    pcol,
    pre,
    bk,
    ga,
    hl,
    scaled,
    dsend,
    drecv,
    dback,
    down,
    pb,
    po,
    pf,
    gsend,
    grecv,
    tsend,
    trecv,
    l_sem,
    m_s,
    m_r,
    raw_s,
    raw_r,
    w_s,
    w_r,
    d_s,
    d_r,
    f_s,
    f_r,
    x_s,
    x_r,
    pb_s,
    pb_r,
    rb_s,
    rb_r,
    g_s,
    g_r,
    t_s,
    t_r,
    pf_s,
    pf_r,
):
    dp = lax.axis_index("dp")
    ex = lax.axis_index("expert")
    y, h = dp // 2, dp % 2
    z, l, c = ex // 4, (ex // 2) % 2, ex % 2
    active = c == h
    base = (y % 2) * 2

    def device(yy, hh, zz, ll, cc):
        return (((yy + 4) % 4) * 2 + hh, ((zz + 4) % 4) * 4 + ll * 2 + cc)

    def remote(src, dst, send, recv, target):
        return pltpu.make_async_remote_copy(
            src_ref=src,
            dst_ref=dst,
            send_sem=send,
            recv_sem=recv,
            device_id=target,
            device_id_type=MESH,
        )

    here = (dp, ex)

    barrier = pltpu.get_barrier_semaphore()
    for n in range(1, 16):
        pl.semaphore_signal(barrier, inc=1, device_id=(dp, (ex + n) % 16), device_id_type=MESH)
    for n in range(1, 8):
        pl.semaphore_signal(barrier, inc=1, device_id=((dp + n) % 8, ex), device_id_type=MESH)

    local = [
        pltpu.make_async_copy(wg.at[0], wgu.at[0, pl.ds(0, FF)], l_sem.at[0]),
        pltpu.make_async_copy(wu.at[0], wgu.at[0, pl.ds(128, FF)], l_sem.at[1]),
        pltpu.make_async_copy(wd.at[0], wdn.at[0, pl.ds(0, FF)], l_sem.at[2]),
    ]
    for copy in local:
        copy.start()

    def quarter_of(ref, q):
        return ref.at[:, pl.ds(pl.multiple_of((base + q) * Q, Q), Q)]

    own_copies = [
        pltpu.make_async_copy(quarter_of(ref, q), xo.at[q, :, pl.ds(i * Q, Q)], l_sem.at[3 + 2 * q + i])
        for q in range(2)
        for i, ref in enumerate((tok, dy))
    ]

    @pl.when(active)
    def _():
        for copy in own_copies:
            copy.start()

    zeros = jnp.zeros((128 - FF, D), BF16)
    for j in range(2):
        wgu[j, FF:128] = zeros
        wgu[j, 128 + FF : 256] = zeros
        wdn[j, FF:128] = zeros
    upper[...] = (
        lax.broadcasted_iota(jnp.int32, (TOK, TOK), 0) < lax.broadcasted_iota(jnp.int32, (TOK, TOK), 1)
    ).astype(F32).astype(BF16)
    slot_iota = lax.broadcasted_iota(jnp.int32, (CAP, TOK), 0).astype(F32)
    eye = (
        lax.broadcasted_iota(jnp.int32, (CAP, 128), 0) == lax.broadcasted_iota(jnp.int32, (CAP, 128), 1)
    ).astype(F32)

    def targets(named):
        before = dot(named.astype(BF16), upper[...])
        return jnp.where(named > 0, before, -1.0)

    def one_hot(target_row):
        return (slot_iota == target_row).astype(F32)

    pl.semaphore_wait(barrier, 22)

    def raw_copy(q, i):
        ref = (tok, dy)[i]
        return remote(
            quarter_of(ref, q),
            raw.at[q, :, pl.ds(i * Q, Q)],
            raw_s.at[2 * q + i],
            raw_r.at[2 * q + i],
            device(y, h, z, 1 - l, c),
        )

    def meta_copy(w, k, cc):
        n = (w * 4 + k) * 2
        return remote(
            meta,
            mb.at[w * 4 + k],
            m_s.at[n + cc],
            m_r.at[w * 4 + k],
            device(y, h, z + k, l if w == 0 else 1 - l, cc),
        )

    def each_peer(w, k, f):
        for cc in range(2):
            if w == 0 and k == 0:

                @pl.when(cc != c)
                def _(cc=cc):
                    f(cc)

            else:
                f(cc)

    def w_copy(n):
        src = (wg, wu, wd)[n]
        dst = (wgu.at[1, pl.ds(0, FF)], wgu.at[1, pl.ds(128, FF)], wdn.at[1, pl.ds(0, FF)])[n]
        return remote(src.at[0], dst, w_s.at[n], w_r.at[n], device(y, 1 - h, z, l, c))

    @pl.when(active)
    def _():
        for w in range(2):
            for k in range(4):
                each_peer(w, k, lambda cc, w=w, k=k: meta_copy(w, k, cc).start())
        for q in range(2):
            for i in range(2):
                raw_copy(q, i).start()

    for n in range(3):
        w_copy(n).start()

    def d_copy(w, k, cc, q):
        n = (w * 4 + k) * 2
        return remote(
            stage.at[w, q, pl.ds((k * 2 + cc) * CAP, CAP)],
            slots.at[base + q, pl.ds((w * 4 + k) * CAP, CAP)],
            d_s.at[(n + cc) * 2 + q],
            d_r.at[n + q],
            device(y, h, z + k, l, cc),
        )

    def f_copy(s, q):
        rows = slots.at[base + q, pl.ds(s * CAP, CAP)]
        return remote(
            rows, rows, f_s.at[2 * s + q], f_r.at[2 * s + q], device(y + (-1 if q == 0 else 1), h, z, l, c)
        )

    def f_wait(s, q):
        rows = slots.at[2 - base + q, pl.ds(s * CAP, CAP)]
        remote(
            rows, rows, f_s.at[2 * s + q], f_r.at[2 * s + q], device(y + (1 if q == 0 else -1), h, z, l, c)
        ).wait_recv()

    order = (1, 3, 2, 0)

    def named_by(ids0, ids1, experts):
        first = (ids0 == experts).astype(F32)
        second = (ids1 == experts).astype(F32)
        return first, second

    def expert_column(count, w0):
        r = lax.broadcasted_iota(jnp.int32, (count, 1), 0) + w0 * 8
        return (4 * ((z + (r // 2) % 4) % 4) + 2 * ((l + r // 8) % 2) + r % 2).astype(F32)

    def dispatch(w, source, chooser):
        for q in range(2):
            stage[w, q] = dot(chooser[0:ROWS, :], source[q]).astype(BF16)
            for k in order:

                def send(cc, k=k, q=q):
                    d_copy(w, k, cc, q).start()

                if k == 0:
                    for cc in range(2):

                        @pl.when(cc != c)
                        def _(cc=cc):
                            send(cc)

                else:
                    for cc in range(2):
                        send(cc)
            slots[base + q, w * 4 * CAP : w * 4 * CAP + CAP] = stage[
                w, q, pl.ds(pl.multiple_of(c * CAP, CAP), CAP)
            ]

    @pl.when(active)
    def _():
        mb[0] = meta[...]
        first, second = named_by(meta[0:1], meta[1:2], expert_column(16, 0))
        where = targets(first + second)
        for r in range(16):
            p_own[r * CAP : (r + 1) * CAP] = one_hot(where[r : r + 1]).astype(BF16)
        for copy in own_copies:
            copy.wait()
        dispatch(0, xo, p_own)
        for q in range(2):
            f_copy(0, q).start()
        meta_copy(1, 0, 0).wait_recv()
        for q in range(2):
            for i in range(2):
                raw_copy(q, i).wait_recv()
        theirs = mb[4]
        first, second = named_by(theirs[0:1], theirs[1:2], expert_column(8, 0))
        where = targets(first + second)
        for r in range(8):
            p_oth[r * CAP : (r + 1) * CAP] = one_hot(where[r : r + 1]).astype(BF16)
        dispatch(1, raw, p_oth)
        for q in range(2):
            f_copy(4, q).start()

    for w in range(2):
        for k in order:
            s = w * 4 + k

            def arrive(w=w, k=k, s=s):
                for q in range(2):
                    d_copy(w, k, 0, q).wait_recv()
                    f_copy(s, q).start()

            if k == 0:
                pl.when(jnp.logical_not(active))(arrive)
            else:
                arrive()

    @pl.when(jnp.logical_not(active))
    def _():
        meta_copy(0, 0, 0).wait_recv()
        meta_copy(1, 0, 0).wait_recv()

    for s in (1, 2, 3, 5, 6, 7):
        meta_copy(s // 4, s % 4, 0).wait_recv()
    mine = jnp.full((1, 1), ex, jnp.int32).astype(F32)
    firsts, seconds = named_by(mb[:, 0, :], mb[:, 1, :], mine)
    where = targets(firsts + seconds)
    weight = firsts * mb[:, 2, :] + seconds * mb[:, 3, :]
    for s in range(8):
        chosen = one_hot(where[s : s + 1]) * weight[s : s + 1]
        column = jnp.sum(chosen, axis=1, keepdims=True)
        pcol[s * CAP : (s + 1) * CAP] = jnp.broadcast_to(column, (CAP, 128))

    for copy in local:
        copy.wait()

    def inward(j, w):
        rows = slice(w * HALF, (w + 1) * HALF)
        acc_gu = jnp.zeros((HALF, 256), F32)
        acc_d = jnp.zeros((HALF, 128), F32)
        for q in range(4):
            acc_gu += dot_nt(slots[q, rows, 0:Q], wgu[j, :, q * Q : (q + 1) * Q])
            acc_d += dot_nt(slots[q, rows, Q : 2 * Q], wdn[j, :, q * Q : (q + 1) * Q])
        pre[j, rows] = acc_gu
        bk[j, rows] = acc_d

    for w in range(2):
        for k in order:
            for q in range(2):
                f_wait(w * 4 + k, q)
        rows = slice(w * HALF, (w + 1) * HALF)
        for q in range(4):
            scaled[q, rows] = (slots[q, rows, Q : 2 * Q].astype(F32) * pcol[rows, 0:1]).astype(BF16)
        inward(0, w)

    for n in range(3):
        w_copy(n).wait_recv()

    def x_copy(w, n):
        step = (1, -1, 2)[n]
        rows = pl.ds(w * HALF, HALF)
        return remote(
            dsend.at[(y + step + 4) % 4, rows],
            drecv.at[(1, 0, 2)[n], rows],
            x_s.at[w * 3 + n],
            x_r.at[w * 3 + (1, 0, 2)[n]],
            device(y + step, h, z, l, c),
        )

    def pb_copy(w, k):
        s = w * 4 + k
        r = w * 8 + k * 2 + c
        return remote(
            pb.at[s], po.at[r], pb_s.at[s], pb_r.at[r], device(y, h, z - k, l if w == 0 else 1 - l, h)
        )

    for w in range(2):
        inward(1, w)
        for half in range(2):
            rows = slice(w * HALF + half * 128, w * HALF + half * 128 + 128)
            total = jnp.zeros((128, 128), F32)
            for j in range(2):
                gate = pre[j, rows, 0:128]
                up = pre[j, rows, 128:256]
                backed = bk[j, rows]
                sig = jax.nn.sigmoid(gate)
                act = gate * sig
                hidden = act * up
                total += hidden * backed
                back = backed * pcol[rows]
                ga[j, rows, 0:128] = (back * up * sig * (1.0 + gate * (1.0 - sig))).astype(BF16)
                ga[j, rows, 128:256] = (back * act).astype(BF16)
                hl[j, rows] = hidden.astype(BF16)
            column = jnp.sum(total, axis=1, keepdims=True)
            for n in range(2):
                s = w * 4 + half * 2 + n
                row = jnp.sum(eye * column[n * CAP : (n + 1) * CAP], axis=0, keepdims=True)
                pb[s] = jnp.broadcast_to(row, (8, 128))
        rows = slice(w * HALF, (w + 1) * HALF)
        for q in range(4):
            part = dot(ga[0, rows], wgu[0, :, q * Q : (q + 1) * Q]) + dot(
                ga[1, rows], wgu[1, :, q * Q : (q + 1) * Q]
            )
            dsend[q, rows] = part.astype(BF16)
        for n in range(3):
            x_copy(w, n).start()
        for k in order:
            if w == 0 and k == 0:
                pl.when(jnp.logical_not(active))(lambda: pb_copy(0, 0).start())
            else:
                pb_copy(w, k).start()

    def g_copy(q):
        return remote(gsend.at[q], grecv.at[q], g_s.at[q], g_r.at[q], device(y, 1 - h, z, l, c))

    for q in range(4):
        part = dot_tn(ga[1], slots[q, :, 0:Q]).astype(BF16)
        gsend[q, 0] = part[0:FF]
        gsend[q, 1] = part[128 : 128 + FF]
        gsend[q, 2] = dot_tn(hl[1], scaled[q]).astype(BF16)[0:FF]
        g_copy(q).start()
    for q in range(4):
        lanes = slice(q * Q, (q + 1) * Q)
        part = dot_tn(ga[0], slots[q, :, 0:Q])
        o_g[0, :, lanes] = part[0:FF]
        o_u[0, :, lanes] = part[128 : 128 + FF]
        o_d[0, :, lanes] = dot_tn(hl[0], scaled[q])[0:FF]

    def rb_copy(w, k):
        s = w * 4 + k
        r = w * 8 + k * 2 + c
        return remote(
            dback.at[pl.ds(s * CAP, CAP)],
            down.at[pl.ds(pl.multiple_of(r * CAP, CAP), CAP)],
            rb_s.at[s],
            rb_r.at[r],
            device(y, h, z - k, l if w == 0 else 1 - l, h),
        )

    for w in range(2):
        for n in range(3):
            x_copy(w, n).wait_recv()
        rows = slice(w * HALF, (w + 1) * HALF)
        total = dsend[y, rows].astype(F32)
        for n in range(3):
            total += drecv[n, rows].astype(F32)
        dback[rows] = total.astype(BF16)
        for k in order:
            if w == 0 and k == 0:
                pl.when(jnp.logical_not(active))(lambda: rb_copy(0, 0).start())
            else:
                rb_copy(w, k).start()

    def pf_copy(n):
        step, hh = n % 4, n // 4
        return remote(
            pf.at[0],
            pf.at[(4 - step) % 4 if n != 4 else 0],
            pf_s.at[n],
            pf_r.at[(4 - step) % 4],
            device(y + step, h if hh == 0 else 1 - h, z, l, c),
        )

    def t_copy():
        return remote(tsend, trecv, t_s.at[0], t_r.at[0], device(y, 1 - h, z, l, c))

    def owner_recv(copy):
        for w in range(2):
            for k in range(4):
                for cc in range(2):
                    r = w * 8 + k * 2 + cc

                    def wait(r=r):
                        copy(r).wait_recv()

                    if w == 0 and k == 0:
                        pl.when(cc != c)(wait)
                    else:
                        wait()

    @pl.when(active)
    def _():
        po[c] = pb[0]
        owner_recv(lambda r: remote(pb.at[0], po.at[r], pb_s.at[0], pb_r.at[r], device(y, 1 - h, z, l, c)))
        first, second = named_by(meta[0:1], meta[1:2], expert_column(16, 0))
        sums = [jnp.zeros((1, TOK), F32), jnp.zeros((1, TOK), F32)]
        for r in range(16):
            column = jnp.sum(eye * po[r, 0:1, :], axis=1, keepdims=True)
            row = jnp.sum(p_own[r * CAP : (r + 1) * CAP].astype(F32) * column, axis=0, keepdims=True)
            sums[0] += row * first[r : r + 1]
            sums[1] += row * second[r : r + 1]
        pf[0] = jnp.concatenate(sums + [jnp.zeros((6, TOK), F32)], axis=0)
        for n in range(1, 8):
            pf_copy(n).start()
        down[pl.ds(pl.multiple_of(c * CAP, CAP), CAP)] = dback[0:CAP]
        owner_recv(
            lambda r: remote(
                dback.at[pl.ds(0, CAP)],
                down.at[pl.ds(r * CAP, CAP)],
                rb_s.at[0],
                rb_r.at[r],
                device(y, 1 - h, z, l, c),
            )
        )
        grad = dot_tn(p_own[...], down[...])
        near, far = grad[:, 0:256], grad[:, 256:512]
        low = h == 0
        tsend[...] = jnp.where(low, far, near).astype(BF16)
        t_copy().start()
        o_tok[...] = jnp.where(low, near, far)

    @pl.when(jnp.logical_not(active))
    def _():
        t_copy().wait_recv()
        o_tok[...] = trecv[...].astype(F32)
        pf_copy(4).wait_recv()

    for n in (1, 2, 3):
        remote(pf.at[0], pf.at[n], pf_s.at[n], pf_r.at[n], device(y + n, h, z, l, c)).wait_recv()
    o_prob[...] = pf[0] + pf[1] + pf[2] + pf[3]

    for q in range(4):
        g_copy(q).wait_recv()
        lanes = slice(q * Q, (q + 1) * Q)
        for n, out in enumerate((o_g, o_u, o_d)):
            out[0, :, lanes] = out[0, :, lanes] + grecv[q, n].astype(F32)

    @pl.when(active)
    def _():
        for w in range(2):
            for k in range(4):
                each_peer(w, k, lambda cc, w=w, k=k: meta_copy(w, k, cc).wait_send())
                for q in range(2):
                    for cc in range(2):
                        if k == 0:
                            pl.when(cc != c)(lambda w=w, k=k, cc=cc, q=q: d_copy(w, k, cc, q).wait_send())
                        else:
                            d_copy(w, k, cc, q).wait_send()
        for q in range(2):
            for i in range(2):
                raw_copy(q, i).wait_send()
        for n in range(1, 8):
            pf_copy(n).wait_send()
        t_copy().wait_send()

    for n in range(3):
        w_copy(n).wait_send()
    for s in range(8):
        for q in range(2):
            f_copy(s, q).wait_send()
    for w in range(2):
        for n in range(3):
            x_copy(w, n).wait_send()
        for k in range(4):

            def sent(w=w, k=k):
                pb_copy(w, k).wait_send()
                rb_copy(w, k).wait_send()

            if w == 0 and k == 0:
                pl.when(jnp.logical_not(active))(sent)
            else:
                sent()
    for q in range(4):
        g_copy(q).wait_send()


def on_device(tokens, out_grad, expert_ids, gate_probs, w_gate, w_up, w_down):
    meta = jnp.concatenate(
        [expert_ids.T.astype(F32), gate_probs.T.astype(F32), jnp.zeros((4, TOK), F32)], axis=0
    )
    dma = pltpu.SemaphoreType.DMA
    anywhere = pl.BlockSpec(memory_space=pl.ANY)
    vmem = pl.BlockSpec(memory_space=pltpu.VMEM)
    token_grad, prob, grad_gate, grad_up, grad_down = pl.pallas_call(
        kernel,
        out_shape=(
            jax.ShapeDtypeStruct((TOK, 256), F32),
            jax.ShapeDtypeStruct((8, TOK), F32),
            jax.ShapeDtypeStruct((1, FF, D), F32),
            jax.ShapeDtypeStruct((1, FF, D), F32),
            jax.ShapeDtypeStruct((1, FF, D), F32),
        ),
        in_specs=[anywhere, anywhere, vmem, anywhere, anywhere, anywhere],
        out_specs=(vmem,) * 5,
        scratch_shapes=[
            pltpu.VMEM((8, 8, TOK), F32),
            pltpu.VMEM((2, TOK, 2 * Q), BF16),
            pltpu.VMEM((2, TOK, 2 * Q), BF16),
            pltpu.VMEM((2, 2, ROWS, 2 * Q), BF16),
            pltpu.VMEM((4, ROWS, 2 * Q), BF16),
            pltpu.VMEM((2, 256, D), BF16),
            pltpu.VMEM((2, 128, D), BF16),
            pltpu.VMEM((TOK, TOK), BF16),
            pltpu.VMEM((16 * CAP, TOK), BF16),
            pltpu.VMEM((8 * CAP, TOK), BF16),
            pltpu.VMEM((ROWS, 128), F32),
            pltpu.VMEM((2, ROWS, 256), F32),
            pltpu.VMEM((2, ROWS, 128), F32),
            pltpu.VMEM((2, ROWS, 256), BF16),
            pltpu.VMEM((2, ROWS, 128), BF16),
            pltpu.VMEM((4, ROWS, Q), BF16),
            pltpu.VMEM((4, ROWS, Q), BF16),
            pltpu.VMEM((3, ROWS, Q), BF16),
            pltpu.VMEM((ROWS, Q), BF16),
            pltpu.VMEM((16 * CAP, Q), BF16),
            pltpu.VMEM((8, 8, 128), F32),
            pltpu.VMEM((16, 8, 128), F32),
            pltpu.VMEM((4, 8, TOK), F32),
            pltpu.VMEM((4, 3, FF, Q), BF16),
            pltpu.VMEM((4, 3, FF, Q), BF16),
            pltpu.VMEM((TOK, 256), BF16),
            pltpu.VMEM((TOK, 256), BF16),
            dma((7,)),
            dma((16,)),
            dma((8,)),
            dma((4,)),
            dma((4,)),
            dma((3,)),
            dma((3,)),
            dma((32,)),
            dma((16,)),
            dma((16,)),
            dma((16,)),
            dma((6,)),
            dma((6,)),
            dma((8,)),
            dma((16,)),
            dma((8,)),
            dma((16,)),
            dma((4,)),
            dma((4,)),
            dma((1,)),
            dma((1,)),
            dma((8,)),
            dma((4,)),
        ],
        compiler_params=pltpu.CompilerParams(
            collective_id=0, has_side_effects=True, vmem_limit_bytes=48 << 20
        ),
        name="expert_backward",
    )(tokens, out_grad, meta, w_gate, w_up, w_down)
    return token_grad, prob[0:2].T, grad_gate, grad_up, grad_down


def solution(mesh):
    in_specs = (
        P("expert", None),
        P("expert", None),
        P("expert", None),
        P("expert", None),
        P("expert", "dp", None),
        P("expert", "dp", None),
        P("expert", "dp", None),
    )
    out_specs = (
        P("expert", "dp"),
        P("expert", None),
        P("expert", "dp", None),
        P("expert", "dp", None),
        P("expert", "dp", None),
    )
    return jax.shard_map(
        on_device, mesh=mesh, in_specs=in_specs, out_specs=out_specs, check_vma=False
    )
```

time: 669 us -> 112 us (0.17)
  waiting for transfers between devices: 508 us -> 0 us
  Pallas kernels: 0 us -> 99.8 us
  other arithmetic: 42.6 us -> 0.08 us
  blocking collectives: 36.5 us -> 0 us
  matrix products: 35.9 us -> 0 us
  local copies, waits for them, and re-layouts: 30.8 us -> 10.7 us
  between operations: 14.1 us -> 0.67 us
    unnamed x6 -> x0, waiting for transfers between devices: 408 us -> none
    pallas_call x0 -> x1, Pallas kernels: none -> 99.8 us  [on_device(): pl.pallas_call(kernel, out_shape=(jax.ShapeDtypeStruct((TOK, 256), F32),...]
    all_gather x3 -> x0, waiting for transfers between devices: 94.4 us -> none  [the longest x1 38.5 us: on_device(): part_down = lax.all_gather(w_down, 'expert', axis=0, tiled=True)]
    psum x1 -> x0, blocking collectives: 36.5 us -> none  [on_device(): prob_grad = lax.psum(prob_sum.reshape(rows_here, top_count), 'dp')]
    dot_general x8 -> x0, matrix products: 35.9 us -> none  [the longest x3 19.7 us: inward(): jnp.einsum('ecd,' + weight_form + '->ecf', values, weight, preferred_elem...]
    scatter-add x2 -> x0, other arithmetic: 23 us -> none  [the longest x1 15.4 us: on_device(): dx_sum.at[(slot_index // top_count).reshape(-1)]]
    gather x4 -> x0, local copies, waits for them, and re-layouts: 18.9 us -> none  [the longest x2 6.88 us: on_device(): slot_p = gate_probs.reshape(-1)[slot_index] * filled.astype(jnp.bfloat16)]
    another operation x3 -> x0, other arithmetic: 13.8 us -> none  [the longest x1 12.6 us: on_device(): stacked = jnp.stack(partials, axis=1).astype(jnp.bfloat16)]
  transfers between devices with their start and end apart: 5 -> 0, of which waited for: 5 -> 0; matrix products, arithmetic and copies ran while one was open for 11% -> 0% of each run, Pallas kernels for 0% -> 0%
where the time goes in v1:
time: 112 us; the launch traced here: 111 us
  Pallas kernels  99.8 us (89%)
  local copies, waits for them, and re-layouts  10.7 us (10%)
    pallas_call x1, Pallas kernels, on_device(): pl.pallas_call(kernel, out_shape=(jax.ShapeDtypeStruct((TOK, 256), F32),...  99.8 us
    unnamed x18, local copies, waits for them, and re-layouts  10 us

profile of v1, /device:TPU:1, one launch (start us, length us, event | category | flops | bytes accessed | tf_op | source)
XLA Modules:
  0.0 111.3 jit_solution(14493338788589221882)
XLA Ops:
  0.6 0.0 copy-start.5
  0.7 0.1 pad.2.clone
  0.7 0.6 copy-done.5
  1.3 0.0 copy-start.6
  1.3 0.7 copy-done.6
  2.0 0.1 maximum_maximum_fusion.meta
  2.1 0.0 copy-start
  2.1 1.2 %copy-done = bf16[256,2048]{1,0:T(8,128)(2,1)S(1)} copy-done((bf16[256,2048]{1,0:T(8,128)(2,1)S(1)}, bf16[256,2048]{1,0:T(8,128)(2,1)}, u32[]{:S(2)}) %copy-start) | copy-done | bytes 1048600
  3.3 0.0 copy-start.1
  3.3 1.2 %copy-done.1 = bf16[256,2048]{1,0:T(8,128)(2,1)S(1)} copy-done((bf16[256,2048]{1,0:T(8,128)(2,1)S(1)}, bf16[256,2048]{1,0:T(8,128)(2,1)}, u32[]{:S(2)}) %copy-start.1) | copy-done | bytes 1048600
  4.5 0.0 copy-start.2
  4.5 1.0 copy-done.2
  5.5 0.0 copy-start.3
  5.5 1.0 copy-done.3
  6.5 0.0 copy-start.4
  6.5 1.0 copy-done.4
  7.5 99.8 %expert_backward.1 = (f32[256,256]{1,0:T(8,128)S(1)}, f32[8,256]{1,0:T(8,128)S(1)}, f32[1,96,2048]{2,1,0:T(8,128)S(1)}, f32[1,96,2048]{2,1,0:T(8,128)S(1)}, f32[1,96,2048]{2,1,0:T(8,128)S(1)}) custom-call(bf16[256,2048]{1,0:T(8,128)(2,1)S(1)} %copy-done, bf16[256,2048]{1,0:T(8,128)(2,1)S(1)} %copy-done.1, f32[8,256]{1,0:T(8,128)S(1)} %maximum_maximum_fusion.meta, ...), custom_call_target="tpu_custom_call" | custom-call | tf_op jit(solution)/shard_map/expert_backward/pallas_call | solution.py:567
  107.3 0.6 slice_bitcast_fusion
  107.9 0.7 copy.16
  108.6 0.9 copy.17
  109.5 0.9 copy.18
  110.4 0.9 copy.19
  (3 shorter events, 0.0 us)
Async XLA Ops:
  0.6 0.7 copy-start.5
  1.3 0.7 copy-start.6
  2.1 1.2 %copy-start = (bf16[256,2048]{1,0:T(8,128)(2,1)S(1)}, bf16[256,2048]{1,0:T(8,128)(2,1)}, u32[]{:S(2)}) copy-start(bf16[256,2048]{1,0:T(8,128)(2,1)} %tok.1) | copy-start | bytes 3145732
  3.3 1.2 %copy-start.1 = (bf16[256,2048]{1,0:T(8,128)(2,1)S(1)}, bf16[256,2048]{1,0:T(8,128)(2,1)}, u32[]{:S(2)}) copy-start(bf16[256,2048]{1,0:T(8,128)(2,1)} %dy.1) | copy-start | bytes 3145732
  4.5 1.0 copy-start.2
  5.5 1.0 copy-start.3
  6.5 1.0 copy-start.4

commit v2 on v1

v2 whole, which is shorter than its diff:
```python
import jax
import jax.numpy as jnp
from jax import lax
from jax.experimental import pallas as pl
from jax.experimental.pallas import tpu as pltpu
from jax.sharding import PartitionSpec as P

MESH = pl.DeviceIdType.MESH
F32 = jnp.float32
BF16 = jnp.bfloat16

D = 2048
FF = 96
TOK = 256
CAP = 64
Q = 512
ROWS = 8 * CAP
HALF = ROWS // 2


def dot(a, b):
    return jnp.dot(a, b, preferred_element_type=F32)


def dot_nt(a, b):
    return lax.dot_general(a, b, (((1,), (1,)), ((), ())), preferred_element_type=F32)


def dot_tn(a, b):
    return lax.dot_general(a, b, (((0,), (0,)), ((), ())), preferred_element_type=F32)


def kernel(
    tok,
    dy,
    ids,
    prob,
    wg,
    wu,
    wd,
    o_tok,
    o_prob,
    o_g,
    o_u,
    o_d,
    meta,
    mb,
    xo,
    raw,
    stage,
    stage_oth,
    slots,
    wgu,
    wdn,
    upper,
    p_own,
    p_back,
    p_oth,
    pcol,
    pre,
    bk,
    ga,
    ga_t,
    hl_t,
    psum,
    scaled,
    dacc,
    dsend,
    far,
    near,
    csend,
    chain,
    dback,
    down,
    pb,
    po,
    pf,
    gd_send,
    gd_recv,
    gsend,
    grecv,
    tsend,
    trecv,
    l_sem,
    m_s,
    m_r,
    raw_s,
    raw_r,
    w_s,
    w_r,
    d_s,
    d_r,
    f_s,
    f_r,
    e_s,
    e_r,
    v_s,
    v_r,
    far_s,
    far_r,
    near_s,
    near_r,
    ch_s,
    ch_r,
    pb_s,
    pb_r,
    rb_s,
    rb_r,
    gd_s,
    gd_r,
    g_s,
    g_r,
    t_s,
    t_r,
    pf_s,
    pf_r,
):
    dp = lax.axis_index("dp")
    ex = lax.axis_index("expert")
    y, h = dp // 2, dp % 2
    z, l, c = ex // 4, (ex // 2) % 2, ex % 2
    active = c == h
    idle = jnp.logical_not(active)
    base = (y % 2) * 2

    def device(yy, hh, zz, ll, cc):
        return (((yy + 4) % 4) * 2 + hh, ((zz + 4) % 4) * 4 + ll * 2 + cc)

    def remote(src, dst, send, recv, target):
        return pltpu.make_async_remote_copy(
            src_ref=src,
            dst_ref=dst,
            send_sem=send,
            recv_sem=recv,
            device_id=target,
            device_id_type=MESH,
        )

    def other(w):
        return l if w == 0 else 1 - l

    barrier = pltpu.get_barrier_semaphore()
    for n in range(1, 16):
        pl.semaphore_signal(barrier, inc=1, device_id=(dp, (ex + n) % 16), device_id_type=MESH)
    for n in range(1, 8):
        pl.semaphore_signal(barrier, inc=1, device_id=((dp + n) % 8, ex), device_id_type=MESH)

    local = [
        pltpu.make_async_copy(wg.at[0], wgu.at[0, pl.ds(0, FF)], l_sem.at[0]),
        pltpu.make_async_copy(wu.at[0], wgu.at[0, pl.ds(128, FF)], l_sem.at[1]),
        pltpu.make_async_copy(wd.at[0], wdn.at[0, pl.ds(0, FF)], l_sem.at[2]),
    ]

    def quarter_of(ref, q):
        return ref.at[:, pl.ds(pl.multiple_of((base + q) * Q, Q), Q)]

    own_copies = [
        pltpu.make_async_copy(quarter_of(ref, q), xo.at[q, :, pl.ds(i * Q, Q)], l_sem.at[3 + 2 * q + i])
        for q in range(2)
        for i, ref in enumerate((tok, dy))
    ]

    @pl.when(active)
    def _():
        for copy in own_copies:
            copy.start()

    for copy in local:
        copy.start()
    meta[...] = jnp.concatenate(
        [ids[...].astype(F32), prob[...].astype(F32), jnp.zeros((4, TOK), F32)], axis=0
    )
    zeros = jnp.zeros((128 - FF, D), BF16)
    for j in range(2):
        wgu[j, FF:128] = zeros
        wgu[j, 128 + FF : 256] = zeros
        wdn[j, FF:128] = zeros
    upper[...] = (
        lax.broadcasted_iota(jnp.int32, (TOK, TOK), 0) < lax.broadcasted_iota(jnp.int32, (TOK, TOK), 1)
    ).astype(F32).astype(BF16)
    slot_iota = lax.broadcasted_iota(jnp.int32, (CAP, TOK), 0).astype(F32)
    eye = (
        lax.broadcasted_iota(jnp.int32, (CAP, 128), 0) == lax.broadcasted_iota(jnp.int32, (CAP, 128), 1)
    ).astype(F32)

    def targets(named):
        before = dot(named.astype(BF16), upper[...])
        return jnp.where(named > 0, before, -1.0)

    def one_hot(target_row):
        return (slot_iota == target_row).astype(F32)

    def named_by(ids0, ids1, experts):
        return (ids0 == experts).astype(F32), (ids1 == experts).astype(F32)

    def expert_column(count):
        r = lax.broadcasted_iota(jnp.int32, (count, 1), 0)
        return (4 * ((z + (r // 2) % 4) % 4) + 2 * ((l + r // 8) % 2) + r % 2).astype(F32)

    @pl.when(active)
    def _():
        mb[0] = meta[...]
        first, second = named_by(meta[0:1], meta[1:2], expert_column(16))
        where = targets(first + second)
        for r in range(16):
            p_own[r * CAP : (r + 1) * CAP] = one_hot(where[r : r + 1]).astype(BF16)

    pl.semaphore_wait(barrier, 22)

    def raw_copy(i):
        return remote(
            (tok, dy)[i].at[:, pl.ds(pl.multiple_of(y * Q, Q), Q)],
            raw.at[:, pl.ds(i * Q, Q)],
            raw_s.at[i],
            raw_r.at[i],
            device(y, h, z, 1 - l, c),
        )

    def meta_copy(w, k, cc):
        n = (w * 4 + k) * 2
        return remote(
            meta, mb.at[w * 4 + k], m_s.at[n + cc], m_r.at[w * 4 + k], device(y, h, z + k, other(w), cc)
        )

    def w_copy(n):
        src = (wg, wu, wd)[n]
        dst = (wgu.at[1, pl.ds(0, FF)], wgu.at[1, pl.ds(128, FF)], wdn.at[1, pl.ds(0, FF)])[n]
        return remote(src.at[0], dst, w_s.at[n], w_r.at[n], device(y, 1 - h, z, l, c))

    def each_peer(k, f):
        for cc in range(2):
            if k == 0:
                pl.when(cc != c)(lambda cc=cc: f(cc))
            else:
                f(cc)

    def each_meta(f):
        for w in range(2):
            for k in range(4):
                each_peer(k if w == 0 else 4, lambda cc, w=w, k=k: f(meta_copy(w, k, cc)))

    order = (1, 3, 2)

    def d_copy(w, k, cc, q):
        n = w * 16 + (k * 2 + cc) * 2 + q
        m = w * 8 + k * 2 + q
        rows = pl.ds((k * 2 + cc) * CAP, CAP)
        into = pl.ds((w * 4 + k) * CAP, CAP)
        return remote(
            stage.at[q, rows] if w == 0 else stage_oth.at[q, rows],
            slots.at[base + q, into] if w == 0 else slots.at[y, into, pl.ds(q * Q, Q)],
            d_s.at[n],
            d_r.at[m],
            device(y, h, z + k, l, cc),
        )

    def f_rows(k, q, up, quarter):
        return slots.at[quarter, pl.ds(k * CAP + 32 * ((up + q + 1) % 2), 32)]

    def f_copy(k, q, up):
        n = (2 * k + q) * 2 + up
        rows = f_rows(k, q, up, base + q)
        return remote(rows, rows, f_s.at[n], f_r.at[n], device(y + (1 if up else -1), h, z, l, c))

    def f_wait(k, q, up):
        n = (2 * k + q) * 2 + up
        rows = f_rows(k, q, up, 2 - base + q)
        remote(rows, rows, f_s.at[n], f_r.at[n], device(y + (1 if up else -1), h, z, l, c)).wait_recv()

    def e_copy(k, i, up, quarter):
        n = (2 * k + i) * 2 + up
        rows = slots.at[quarter, pl.ds((4 + k) * CAP, CAP), pl.ds(i * Q, Q)]
        return remote(rows, rows, e_s.at[n], e_r.at[n], device(y + (1 if up else -1), h, z, l, c))

    def v_copy(k, i, up, quarter):
        n = (2 * k + i) * 2 + up
        rows = slots.at[quarter, pl.ds((4 + k) * CAP + 32 * up, 32), pl.ds(i * Q, Q)]
        return remote(rows, rows, v_s.at[n], v_r.at[n], device(y + (1 if up else -1), h, z, l, c))

    everyone = (0,) + order

    def forward(q, which):
        for k in which:
            d_copy(0, k, 0, q).wait_recv()
            for up in range(2):
                f_copy(k, q, up).start()

    def spread(i, which):
        for k in which:
            d_copy(1, k, 0, i).wait_recv()
            for up in range(2):
                e_copy(k, i, up, y).start()

    def pass_on(i):
        for k in everyone:
            for up in range(2):
                quarter = (y + (3 if up else 1)) % 4
                e_copy(k, i, up, quarter).wait_recv()
                v_copy(k, i, up, quarter).start()

    def send_out(w, q, which):
        for k in which:
            each_peer(k, lambda cc, k=k: d_copy(w, k, cc, q).start())

    mine_rows = pl.ds(pl.multiple_of(c * CAP, CAP), CAP)

    def other_block(i):
        raw_copy(i).wait_recv()
        lanes = slice(i * Q, (i + 1) * Q)
        stage_oth[i] = dot(p_oth[...], raw[:, lanes]).astype(BF16)
        send_out(1, i, order + (0,))
        slots[y, 4 * CAP : 5 * CAP, lanes] = stage_oth[i, mine_rows]
        for up in range(2):
            e_copy(0, i, up, y).start()

    @pl.when(active)
    def _():
        raw_copy(0).start()
        each_meta(lambda copy: copy.start())
        for copy in own_copies:
            copy.wait()
        for q in range(2):
            stage[q] = dot(p_own[0:ROWS, :], xo[q]).astype(BF16)
            if q == 0:
                send_out(0, 0, order)
            send_out(0, q, (0,))
            slots[base + q, 0:CAP] = stage[q, mine_rows]
            for up in range(2):
                f_copy(0, q, up).start()
        raw_copy(0).wait_send()
        raw_copy(1).start()
        meta_copy(1, 0, 0).wait_recv()
        theirs = mb[4]
        first, second = named_by(theirs[0:1], theirs[1:2], expert_column(8))
        where = targets(first + second)
        for r in range(8):
            p_oth[r * CAP : (r + 1) * CAP] = one_hot(where[r : r + 1]).astype(BF16)
        other_block(0)
        forward(0, order)
        other_block(1)
        raw_copy(1).wait_send()
        for n in range(3):
            w_copy(n).start()

    @pl.when(idle)
    def _():
        for q in range(2):
            forward(q, (0,))
        spread(0, (0,))
        forward(0, order)
        for n in range(3):
            w_copy(n).start()
        spread(1, (0,))

    spread(0, order)

    @pl.when(active)
    def _():
        send_out(0, 1, order)

    spread(1, order)
    pass_on(0)
    forward(1, order)
    pass_on(1)

    @pl.when(idle)
    def _():
        meta_copy(0, 0, 0).wait_recv()
        meta_copy(1, 0, 0).wait_recv()

    for s in (1, 2, 3, 5, 6, 7):
        meta_copy(s // 4, s % 4, 0).wait_recv()
    mine = jnp.full((1, 1), ex, jnp.int32).astype(F32)
    firsts, seconds = named_by(mb[:, 0, :], mb[:, 1, :], mine)
    where = targets(firsts + seconds)
    weight = firsts * mb[:, 2, :] + seconds * mb[:, 3, :]
    for s in range(8):
        chosen = one_hot(where[s : s + 1]) * weight[s : s + 1]
        column = jnp.sum(chosen, axis=1, keepdims=True)
        pcol[s * CAP : (s + 1) * CAP] = jnp.broadcast_to(column, (CAP, 128))

    for copy in local:
        copy.wait()

    def inward_gu(j, w):
        rows = slice(w * HALF, (w + 1) * HALF)
        acc = jnp.zeros((HALF, 256), F32)
        for q in range(4):
            acc += dot_nt(slots[q, rows, 0:Q], wgu[j, :, q * Q : (q + 1) * Q])
        pre[j, rows] = acc

    def inward_d(j, w):
        rows = slice(w * HALF, (w + 1) * HALF)
        acc = jnp.zeros((HALF, 128), F32)
        for q in range(4):
            acc += dot_nt(slots[q, rows, Q : 2 * Q], wdn[j, :, q * Q : (q + 1) * Q])
        bk[j, rows] = acc

    def hidden_of(j, rows):
        gate = pre[j, rows, 0:128]
        up = pre[j, rows, 128:256]
        sig = jax.nn.sigmoid(gate)
        act = gate * sig
        return gate, up, sig, act, act * up

    def hidden_grads(j, rows):
        gate, up, sig, act, hidden = hidden_of(j, rows)
        backed = bk[j, rows]
        back = backed * pcol[rows]
        g_gate = back * up * sig * (1.0 + gate * (1.0 - sig))
        g_up = back * act
        ga[j, rows, 0:128] = g_gate.astype(BF16)
        ga[j, rows, 128:256] = g_up.astype(BF16)
        ga_t[j, 0:128, rows] = g_gate.T.astype(BF16)
        ga_t[j, 128:256, rows] = g_up.T.astype(BF16)
        return hidden, hidden * backed

    chunks = [slice(n * 128, n * 128 + 128) for n in range(4)]

    for w in range(2):
        for k in everyone:
            for i in range(2):
                for up in range(2):
                    if w == 0:
                        f_wait(k, i, up)
                    else:
                        v_copy(k, i, up, (y + 2) % 4).wait_recv()
        rows = slice(w * HALF, (w + 1) * HALF)
        for q in range(4):
            scaled[q, rows] = (slots[q, rows, Q : 2 * Q].astype(F32) * pcol[rows, 0:1]).astype(BF16)
        inward_gu(0, w)
        inward_d(0, w)
        for part in chunks[2 * w : 2 * w + 2]:
            hidden, terms = hidden_grads(0, part)
            hl_t[0, :, part] = hidden.T.astype(BF16)
            psum[part] = terms
        for q in range(4):
            dacc[q, rows] = dot(ga[0, rows], wgu[0, :, q * Q : (q + 1) * Q])
    for q in range(4):
        lanes = slice(q * Q, (q + 1) * Q)
        part = dot(ga_t[0], slots[q, :, 0:Q])
        o_g[0, :, lanes] = part[0:FF]
        o_u[0, :, lanes] = part[128 : 128 + FF]
        o_d[0, :, lanes] = dot(hl_t[0], scaled[q])[0:FF]

    @pl.when(active)
    def _():
        p_back[...] = p_own[...].astype(F32).T.astype(BF16)

    def gd_copy():
        return remote(gd_send, gd_recv, gd_s.at[0], gd_r.at[0], device(y, 1 - h, z, l, c))

    def g_copy(q):
        return remote(gsend.at[q], grecv.at[q], g_s.at[q], g_r.at[q], device(y, 1 - h, z, l, c))

    for n in range(2):
        w_copy(n).wait_recv()
    for w in range(2):
        inward_gu(1, w)
    for part in chunks:
        hl_t[1, :, part] = hidden_of(1, part)[4].T.astype(BF16)
    for q in range(4):
        gd_send[:, q * Q : (q + 1) * Q] = dot(hl_t[1], scaled[q]).astype(BF16)[0:FF]
    w_copy(2).wait_recv()
    gd_copy().start()

    def to(step):
        return device(y + step, h, z, l, c)

    def part_of(step, side, n):
        return dsend.at[(y + step + 4) % 4, side, pl.ds(n * 128, 128)]

    def rows_of(ref, side, n):
        return ref.at[side, pl.ds(n * 128, 128)]

    def far_copy(n, side):
        i = 2 * n + side
        return remote(
            part_of(2, side, n), rows_of(far, side, n), far_s.at[i], far_r.at[i], to(-1 if side == 0 else 1)
        )

    def near_copy(n, side):
        i = 2 * n + side
        step = 1 if side == 0 else -1
        return remote(part_of(step, side, n), rows_of(near, side, n), near_s.at[i], near_r.at[i], to(step))

    def chain_copy(n, side):
        i = 2 * n + side
        return remote(
            rows_of(csend, side, n),
            rows_of(chain, side, n),
            ch_s.at[i],
            ch_r.at[i],
            to(-1 if side == 0 else 1),
        )

    def pb_copy(s):
        w, k = s // 4, s % 4
        r = w * 8 + k * 2 + c
        return remote(pb.at[s], po.at[r], pb_s.at[s], pb_r.at[r], device(y, h, z - k, other(w), h))

    def each_owner(s, f):
        if s == 0:
            pl.when(idle)(f)
        else:
            f()

    def relay(n):
        for side in range(2):
            far_copy(n, side).wait_recv()
            step = -1 if side == 0 else 1
            rows = slice(n * 128, n * 128 + 128)
            total = far[side, rows].astype(F32) + dsend[(y + step + 4) % 4, side, rows].astype(F32)
            csend[side, rows] = total.astype(BF16)
            chain_copy(n, side).start()

    for n, part in enumerate(chunks):
        if n % 2 == 0:
            inward_d(1, n // 2)
        terms = hidden_grads(1, part)[1] + psum[part]
        column = jnp.sum(terms, axis=1, keepdims=True)
        for i in range(2):
            s = n * 2 + i
            row = jnp.sum(eye * column[i * CAP : (i + 1) * CAP], axis=0, keepdims=True)
            pb[s] = jnp.broadcast_to(row, (8, 128))
        for q in range(4):
            both = dacc[q, part] + dot(ga[1, part], wgu[1, :, q * Q : (q + 1) * Q])
            low = both.astype(BF16)
            dsend[q, 0, part] = low[:, 0:256]
            dsend[q, 1, part] = low[:, 256:512]
        for side in range(2):
            far_copy(n, side).start()
        for side in range(2):
            near_copy(n, side).start()
        for i in range(2):
            each_owner(n * 2 + i, lambda s=n * 2 + i: pb_copy(s).start())
        if n >= 2:
            relay(n - 2)

    def other_grads(q):
        part = dot(ga_t[1], slots[q, :, 0:Q]).astype(BF16)
        gsend[q, 0] = part[0:FF]
        gsend[q, 1] = part[128 : 128 + FF]
        g_copy(q).start()

    other_grads(0)
    relay(2)
    other_grads(1)
    relay(3)

    def rb_copy(s):
        w, k = s // 4, s % 4
        r = w * 8 + k * 2 + c
        return remote(
            dback.at[:, pl.ds(s * CAP, CAP)],
            down.at[:, pl.ds(pl.multiple_of(r * CAP, CAP), CAP)],
            rb_s.at[s],
            rb_r.at[r],
            device(y, h, z - k, other(w), h),
        )

    for n, part in enumerate(chunks):
        for side in range(2):
            near_copy(n, side).wait_recv()
            chain_copy(n, side).wait_recv()
            total = dsend[y, side, part].astype(F32) + near[side, part].astype(F32)
            dback[side, part] = (total + chain[side, part].astype(F32)).astype(BF16)
        for i in range(2):
            each_owner(n * 2 + i, lambda s=n * 2 + i: rb_copy(s).start())

    for q in (2, 3):
        other_grads(q)

    def add_down():
        gd_copy().wait_recv()
        o_d[0] = o_d[0] + gd_recv[...].astype(F32)

    def add_gate_up(q):
        g_copy(q).wait_recv()
        lanes = slice(q * Q, (q + 1) * Q)
        for n, out in enumerate((o_g, o_u)):
            out[0, :, lanes] = out[0, :, lanes] + grecv[q, n].astype(F32)

    def pf_copy(n):
        step, hh = n % 4, n // 4
        return remote(
            pf.at[0],
            pf.at[(4 - step) % 4],
            pf_s.at[n],
            pf_r.at[(4 - step) % 4],
            device(y + step, h if hh == 0 else 1 - h, z, l, c),
        )

    def t_copy():
        return remote(tsend, trecv, t_s.at[0], t_r.at[0], device(y, 1 - h, z, l, c))

    def owner_recv(w, copy):
        for k in range(4):
            each_peer(k if w == 0 else 4, lambda cc, k=k: copy(w * 8 + k * 2 + cc).wait_recv())

    @pl.when(active)
    def _():
        po[c] = pb[0]
        for w in range(2):
            owner_recv(
                w, lambda r: remote(pb.at[0], po.at[r], pb_s.at[0], pb_r.at[r], device(y, 1 - h, z, l, c))
            )
        first, second = named_by(meta[0:1], meta[1:2], expert_column(16))
        sums = [jnp.zeros((1, TOK), F32), jnp.zeros((1, TOK), F32)]
        for r in range(16):
            column = jnp.sum(eye * po[r, 0:1, :], axis=1, keepdims=True)
            row = jnp.sum(p_own[r * CAP : (r + 1) * CAP].astype(F32) * column, axis=0, keepdims=True)
            sums[0] += row * first[r : r + 1]
            sums[1] += row * second[r : r + 1]
        pf[0] = jnp.concatenate(sums + [jnp.zeros((6, TOK), F32)], axis=0)
        for n in range(1, 8):
            pf_copy(n).start()
        add_down()
        add_gate_up(0)
        add_gate_up(1)
        down[:, pl.ds(pl.multiple_of(c * CAP, CAP), CAP)] = dback[:, 0:CAP]
        sent = jnp.zeros((TOK, 256), F32)
        kept = jnp.zeros((TOK, 256), F32)
        for w in range(2):
            owner_recv(
                w,
                lambda r: remote(
                    dback.at[:, pl.ds(0, CAP)],
                    down.at[:, pl.ds(r * CAP, CAP)],
                    rb_s.at[0],
                    rb_r.at[r],
                    device(y, 1 - h, z, l, c),
                ),
            )
            rows = slice(w * ROWS, (w + 1) * ROWS)
            sent += dot(p_back[:, rows], down[1 - h, rows])
            if w == 1:
                tsend[...] = sent.astype(BF16)
                t_copy().start()
            kept += dot(p_back[:, rows], down[h, rows])
        o_tok[...] = kept

    @pl.when(idle)
    def _():
        add_down()
        add_gate_up(0)
        add_gate_up(1)
        t_copy().wait_recv()
        o_tok[...] = trecv[...].astype(F32)
        pf_copy(4).wait_recv()

    for n in (1, 2, 3):
        remote(pf.at[0], pf.at[n], pf_s.at[n], pf_r.at[n], device(y + n, h, z, l, c)).wait_recv()
    o_prob[...] = (pf[0] + pf[1] + pf[2] + pf[3])[0:2]

    for q in (2, 3):
        add_gate_up(q)

    @pl.when(active)
    def _():
        each_meta(lambda copy: copy.wait_send())
        for w in range(2):
            for q in range(2):
                for k in range(4):
                    each_peer(k, lambda cc, w=w, k=k, q=q: d_copy(w, k, cc, q).wait_send())
        for n in range(1, 8):
            pf_copy(n).wait_send()
        t_copy().wait_send()

    for n in range(3):
        w_copy(n).wait_send()
    for k in range(4):
        for i in range(2):
            for up in range(2):
                f_copy(k, i, up).wait_send()
                e_copy(k, i, up, y).wait_send()
                v_copy(k, i, up, (y + 1) % 4).wait_send()
    for s in range(8):

        def sent_back(s=s):
            pb_copy(s).wait_send()
            rb_copy(s).wait_send()

        each_owner(s, sent_back)
    for n in range(4):
        for side in range(2):
            far_copy(n, side).wait_send()
            near_copy(n, side).wait_send()
            chain_copy(n, side).wait_send()
    gd_copy().wait_send()
    for q in range(4):
        g_copy(q).wait_send()


def copy_out(*refs):
    copies = [pltpu.make_async_copy(refs[n], refs[5 + n], refs[10].at[n]) for n in range(5)]
    for copy in copies:
        copy.start()
    for copy in copies:
        copy.wait()


def in_hbm(value):
    return pltpu.with_memory_space_constraint(value, pltpu.HBM)


def on_device(tokens, out_grad, expert_ids, gate_probs, w_gate, w_up, w_down):
    dma = pltpu.SemaphoreType.DMA
    hbm = pl.BlockSpec(memory_space=pltpu.HBM)
    vmem = pl.BlockSpec(memory_space=pltpu.VMEM)
    outs = pl.pallas_call(
        kernel,
        out_shape=(
            jax.ShapeDtypeStruct((TOK, 256), F32),
            jax.ShapeDtypeStruct((2, TOK), F32),
            jax.ShapeDtypeStruct((1, FF, D), F32),
            jax.ShapeDtypeStruct((1, FF, D), F32),
            jax.ShapeDtypeStruct((1, FF, D), F32),
        ),
        in_specs=[hbm, hbm, vmem, vmem, hbm, hbm, hbm],
        out_specs=(vmem,) * 5,
        scratch_shapes=[
            pltpu.VMEM((8, TOK), F32),
            pltpu.VMEM((8, 8, TOK), F32),
            pltpu.VMEM((2, TOK, 2 * Q), BF16),
            pltpu.VMEM((TOK, 2 * Q), BF16),
            pltpu.VMEM((2, ROWS, 2 * Q), BF16),
            pltpu.VMEM((2, ROWS, Q), BF16),
            pltpu.VMEM((4, ROWS, 2 * Q), BF16),
            pltpu.VMEM((2, 256, D), BF16),
            pltpu.VMEM((2, 128, D), BF16),
            pltpu.VMEM((TOK, TOK), BF16),
            pltpu.VMEM((16 * CAP, TOK), BF16),
            pltpu.VMEM((TOK, 16 * CAP), BF16),
            pltpu.VMEM((8 * CAP, TOK), BF16),
            pltpu.VMEM((ROWS, 128), F32),
            pltpu.VMEM((2, ROWS, 256), F32),
            pltpu.VMEM((2, ROWS, 128), F32),
            pltpu.VMEM((2, ROWS, 256), BF16),
            pltpu.VMEM((2, 256, ROWS), BF16),
            pltpu.VMEM((2, 128, ROWS), BF16),
            pltpu.VMEM((ROWS, 128), F32),
            pltpu.VMEM((4, ROWS, Q), BF16),
            pltpu.VMEM((4, ROWS, Q), F32),
            pltpu.VMEM((4, 2, ROWS, 256), BF16),
            pltpu.VMEM((2, ROWS, 256), BF16),
            pltpu.VMEM((2, ROWS, 256), BF16),
            pltpu.VMEM((2, ROWS, 256), BF16),
            pltpu.VMEM((2, ROWS, 256), BF16),
            pltpu.VMEM((2, ROWS, 256), BF16),
            pltpu.VMEM((2, 16 * CAP, 256), BF16),
            pltpu.VMEM((8, 8, 128), F32),
            pltpu.VMEM((16, 8, 128), F32),
            pltpu.VMEM((4, 8, TOK), F32),
            pltpu.VMEM((FF, D), BF16),
            pltpu.VMEM((FF, D), BF16),
            pltpu.VMEM((4, 2, FF, Q), BF16),
            pltpu.VMEM((4, 2, FF, Q), BF16),
            pltpu.VMEM((TOK, 256), BF16),
            pltpu.VMEM((TOK, 256), BF16),
            dma((7,)),
            dma((16,)),
            dma((8,)),
            dma((2,)),
            dma((2,)),
            dma((3,)),
            dma((3,)),
            dma((32,)),
            dma((16,)),
            dma((16,)),
            dma((16,)),
            dma((16,)),
            dma((16,)),
            dma((16,)),
            dma((16,)),
            dma((8,)),
            dma((8,)),
            dma((8,)),
            dma((8,)),
            dma((8,)),
            dma((8,)),
            dma((8,)),
            dma((16,)),
            dma((8,)),
            dma((16,)),
            dma((1,)),
            dma((1,)),
            dma((4,)),
            dma((4,)),
            dma((1,)),
            dma((1,)),
            dma((8,)),
            dma((4,)),
        ],
        compiler_params=pltpu.CompilerParams(
            collective_id=0, has_side_effects=True, vmem_limit_bytes=48 << 20
        ),
        name="expert_backward",
    )(
        in_hbm(tokens),
        in_hbm(out_grad),
        expert_ids.T,
        gate_probs.T,
        in_hbm(w_gate),
        in_hbm(w_up),
        in_hbm(w_down),
    )
    token_grad, prob, grad_gate, grad_up, grad_down = pl.pallas_call(
        copy_out,
        out_shape=tuple(jax.ShapeDtypeStruct(v.shape, v.dtype) for v in outs),
        in_specs=[pl.BlockSpec(memory_space=pl.ANY)] * 5,
        out_specs=(pl.BlockSpec(memory_space=pl.ANY),) * 5,
        scratch_shapes=[dma((5,))],
        compiler_params=pltpu.CompilerParams(vmem_limit_bytes=1 << 20),
        name="copy_out",
    )(*outs)
    return token_grad, prob.T, grad_gate, grad_up, grad_down


def solution(mesh):
    in_specs = (
        P("expert", None),
        P("expert", None),
        P("expert", None),
        P("expert", None),
        P("expert", "dp", None),
        P("expert", "dp", None),
        P("expert", "dp", None),
    )
    out_specs = (
        P("expert", "dp"),
        P("expert", None),
        P("expert", "dp", None),
        P("expert", "dp", None),
        P("expert", "dp", None),
    )
    return jax.shard_map(
        on_device, mesh=mesh, in_specs=in_specs, out_specs=out_specs, check_vma=False
    )
```

time: 112 us -> 88.6 us (0.79)
  Pallas kernels: 99.8 us -> 87.1 us
  local copies, waits for them, and re-layouts: 10.7 us -> 0.68 us
    pallas_call x1, Pallas kernels: 99.8 us -> 85.6 us  [on_device(): pl.pallas_call(kernel, out_shape=(jax.ShapeDtypeStruct((TOK, 256), F32),...]
    unnamed x18 -> x4, local copies, waits for them, and re-layouts: 10 us -> 0.68 us
    pallas_call x0 -> x1, Pallas kernels: none -> 1.53 us  [on_device(): pl.pallas_call(copy_out, out_shape=tuple((jax.ShapeDtypeStruct(v.shape, v...]
where the time goes in v2:
time: 88.6 us; the launch traced here: 88.5 us
  Pallas kernels  87.1 us (98%)
    pallas_call x1, Pallas kernels, on_device(): pl.pallas_call(kernel, out_shape=(jax.ShapeDtypeStruct((TOK, 256), F32),...  85.6 us

profile of v2, /device:TPU:1, one launch (start us, length us, event | category | flops | bytes accessed | tf_op | source)
XLA Modules:
  0.0 88.5 jit_solution(17151453683957222421)
XLA Ops:
  0.6 0.0 copy-start
  0.6 0.0 copy-start.1
  0.7 0.7 copy-done
  1.3 0.0 copy-done.1
  1.3 85.6 %expert_backward.1 = (f32[256,256]{1,0:T(8,128)S(1)}, f32[2,256]{1,0:T(2,128)S(1)}, f32[1,96,2048]{2,1,0:T(8,128)S(1)}, f32[1,96,2048]{2,1,0:T(8,128)S(1)}, f32[1,96,2048]{2,1,0:T(8,128)S(1)}) custom-call(bf16[256,2048]{1,0:T(8,128)(2,1)} %tok.1, bf16[256,2048]{1,0:T(8,128)(2,1)} %dy.1, s32[2,256]{1,0:T(2,128)S(1)} %bitcast.3, bf16[2,256]{1,0:T(2,128)(2,1)S(1)} %bitcast.4, ...), custom_call_target="tpu_custom_call" | custom-call | tf_op jit(solution)/shard_map/expert_backward/pallas_call | solution.py:711
  86.9 1.5 %copy_out.1 = (f32[256,256]{1,0:T(8,128)}, f32[2,256]{1,0:T(2,128)}, f32[1,96,2048]{2,1,0:T(8,128)}, f32[1,96,2048]{2,1,0:T(8,128)}, f32[1,96,2048]{2,1,0:T(8,128)}) custom-call(f32[256,256]{1,0:T(8,128)S(1)} %get-tuple-element.15.refs_0_, f32[2,256]{1,0:T(2,128)S(1)} %get-tuple-element.16.refs_1_, f32[1,96,2048]{2,1,0:T(8,128)S(1)} %get-tuple-element.17.refs_2_, ...), custom_call_target="tpu_custom_call" | custom-call | tf_op jit(solution)/shard_map/copy_out/pallas_call | solution.py:808
Async XLA Ops:
  0.6 0.7 copy-start
  0.6 0.7 copy-start.1

commit v3 on v2

--- a/solution.py
+++ b/solution.py
@@ -55,6 +55,7 @@
     upper,
     p_own,
     p_back,
+    p_oth_back,
     p_oth,
     pcol,
     pre,
@@ -139,11 +140,14 @@
     def other(w):
         return l if w == 0 else 1 - l
 
+    diagonal = device(y, 1 - h, z, 1 - l, c)
+
     barrier = pltpu.get_barrier_semaphore()
     for n in range(1, 16):
         pl.semaphore_signal(barrier, inc=1, device_id=(dp, (ex + n) % 16), device_id_type=MESH)
     for n in range(1, 8):
         pl.semaphore_signal(barrier, inc=1, device_id=((dp + n) % 8, ex), device_id_type=MESH)
+    pl.semaphore_signal(barrier, inc=1, device_id=diagonal, device_id_type=MESH)
 
     local = [
         pltpu.make_async_copy(wg.at[0], wgu.at[0, pl.ds(0, FF)], l_sem.at[0]),
@@ -151,12 +155,15 @@
         pltpu.make_async_copy(wd.at[0], wdn.at[0, pl.ds(0, FF)], l_sem.at[2]),
     ]
 
+    def own_quarter(q):
+        return (base + q) % 4
+
     def quarter_of(ref, q):
-        return ref.at[:, pl.ds(pl.multiple_of((base + q) * Q, Q), Q)]
+        return ref.at[:, pl.ds(pl.multiple_of(own_quarter(q) * Q, Q), Q)]
 
     own_copies = [
         pltpu.make_async_copy(quarter_of(ref, q), xo.at[q, :, pl.ds(i * Q, Q)], l_sem.at[3 + 2 * q + i])
-        for q in range(2)
+        for q in (1, 0, 2)
         for i, ref in enumerate((tok, dy))
     ]
 
@@ -205,7 +212,7 @@
         for r in range(16):
             p_own[r * CAP : (r + 1) * CAP] = one_hot(where[r : r + 1]).astype(BF16)
 
-    pl.semaphore_wait(barrier, 22)
+    pl.semaphore_wait(barrier, 23)
 
     def raw_copy(i):
         return remote(
@@ -242,30 +249,22 @@
     order = (1, 3, 2)
 
     def d_copy(w, k, cc, q):
-        n = w * 16 + (k * 2 + cc) * 2 + q
-        m = w * 8 + k * 2 + q
+        n = w * 24 + (k * 2 + cc) * 3 + q
+        m = w * 12 + k * 3 + q
         rows = pl.ds((k * 2 + cc) * CAP, CAP)
         into = pl.ds((w * 4 + k) * CAP, CAP)
         return remote(
             stage.at[q, rows] if w == 0 else stage_oth.at[q, rows],
-            slots.at[base + q, into] if w == 0 else slots.at[y, into, pl.ds(q * Q, Q)],
+            slots.at[own_quarter(q), into] if w == 0 else slots.at[y, into, pl.ds(q * Q, Q)],
             d_s.at[n],
             d_r.at[m],
             device(y, h, z + k, l, cc),
         )
 
-    def f_rows(k, q, up, quarter):
-        return slots.at[quarter, pl.ds(k * CAP + 32 * ((up + q + 1) % 2), 32)]
-
-    def f_copy(k, q, up):
-        n = (2 * k + q) * 2 + up
-        rows = f_rows(k, q, up, base + q)
+    def f_copy(k, up, quarter):
+        n = 2 * k + up
+        rows = slots.at[quarter, pl.ds(k * CAP + 32 * up, 32)]
         return remote(rows, rows, f_s.at[n], f_r.at[n], device(y + (1 if up else -1), h, z, l, c))
-
-    def f_wait(k, q, up):
-        n = (2 * k + q) * 2 + up
-        rows = f_rows(k, q, up, 2 - base + q)
-        remote(rows, rows, f_s.at[n], f_r.at[n], device(y + (1 if up else -1), h, z, l, c)).wait_recv()
 
     def e_copy(k, i, up, quarter):
         n = (2 * k + i) * 2 + up
@@ -279,11 +278,11 @@
 
     everyone = (0,) + order
 
-    def forward(q, which):
+    def forward(which):
         for k in which:
-            d_copy(0, k, 0, q).wait_recv()
+            d_copy(0, k, 0, 1).wait_recv()
             for up in range(2):
-                f_copy(k, q, up).start()
+                f_copy(k, up, base + 1).start()
 
     def spread(i, which):
         for k in which:
@@ -313,22 +312,24 @@
         for up in range(2):
             e_copy(0, i, up, y).start()
 
+    def own_block(q):
+        stage[q] = dot(p_own[0:ROWS, :], xo[q]).astype(BF16)
+        slots[own_quarter(q), 0:CAP] = stage[q, mine_rows]
+
     @pl.when(active)
     def _():
         raw_copy(0).start()
         each_meta(lambda copy: copy.start())
         for copy in own_copies:
             copy.wait()
-        for q in range(2):
-            stage[q] = dot(p_own[0:ROWS, :], xo[q]).astype(BF16)
-            if q == 0:
-                send_out(0, 0, order)
-            send_out(0, q, (0,))
-            slots[base + q, 0:CAP] = stage[q, mine_rows]
-            for up in range(2):
-                f_copy(0, q, up).start()
+        own_block(1)
+        send_out(0, 1, order + (0,))
+        for up in range(2):
+            f_copy(0, up, base + 1).start()
         raw_copy(0).wait_send()
         raw_copy(1).start()
+        own_block(0)
+        own_block(2)
         meta_copy(1, 0, 0).wait_recv()
         theirs = mb[4]
         first, second = named_by(theirs[0:1], theirs[1:2], expert_column(8))
@@ -336,32 +337,31 @@
         for r in range(8):
             p_oth[r * CAP : (r + 1) * CAP] = one_hot(where[r : r + 1]).astype(BF16)
         other_block(0)
-        forward(0, order)
+        raw_copy(1).wait_send()
+        for n in range(2):
+            w_copy(n).start()
+        forward(order)
         other_block(1)
-        raw_copy(1).wait_send()
-        for n in range(3):
+
+    @pl.when(idle)
+    def _():
+        forward((0,))
+        spread(0, (0,))
+        for n in range(2):
             w_copy(n).start()
-
-    @pl.when(idle)
-    def _():
-        for q in range(2):
-            forward(q, (0,))
-        spread(0, (0,))
-        forward(0, order)
-        for n in range(3):
-            w_copy(n).start()
+        forward(order)
         spread(1, (0,))
 
     spread(0, order)
 
     @pl.when(active)
     def _():
-        send_out(0, 1, order)
+        for q in (0, 2):
+            send_out(0, q, order + (0,))
 
     spread(1, order)
+    w_copy(2).start()
     pass_on(0)
-    forward(1, order)
-    pass_on(1)
 
     @pl.when(idle)
     def _():
@@ -378,6 +378,8 @@
         chosen = one_hot(where[s : s + 1]) * weight[s : s + 1]
         column = jnp.sum(chosen, axis=1, keepdims=True)
         pcol[s * CAP : (s + 1) * CAP] = jnp.broadcast_to(column, (CAP, 128))
+
+    pass_on(1)
 
     for copy in local:
         copy.wait()
@@ -418,12 +420,18 @@
     chunks = [slice(n * 128, n * 128 + 128) for n in range(4)]
 
     for w in range(2):
-        for k in everyone:
-            for i in range(2):
+        if w == 0:
+            pl.when(idle)(lambda: [d_copy(0, 0, 0, q).wait_recv() for q in (0, 2)][0])
+            for k in order:
+                for q in (0, 2):
+                    d_copy(0, k, 0, q).wait_recv()
+            for k in everyone:
                 for up in range(2):
-                    if w == 0:
-                        f_wait(k, i, up)
-                    else:
+                    f_copy(k, up, 3 - base).wait_recv()
+        else:
+            for k in everyone:
+                for i in range(2):
+                    for up in range(2):
                         v_copy(k, i, up, (y + 2) % 4).wait_recv()
         rows = slice(w * HALF, (w + 1) * HALF)
         for q in range(4):
@@ -436,16 +444,12 @@
             psum[part] = terms
         for q in range(4):
             dacc[q, rows] = dot(ga[0, rows], wgu[0, :, q * Q : (q + 1) * Q])
-    for q in range(4):
-        lanes = slice(q * Q, (q + 1) * Q)
-        part = dot(ga_t[0], slots[q, :, 0:Q])
-        o_g[0, :, lanes] = part[0:FF]
-        o_u[0, :, lanes] = part[128 : 128 + FF]
-        o_d[0, :, lanes] = dot(hl_t[0], scaled[q])[0:FF]
-
-    @pl.when(active)
-    def _():
-        p_back[...] = p_own[...].astype(F32).T.astype(BF16)
+        if w == 0:
+            for n in range(2):
+                w_copy(n).wait_recv()
+        inward_gu(1, w)
+        for part in chunks[2 * w : 2 * w + 2]:
+            hl_t[1, :, part] = hidden_of(1, part)[4].T.astype(BF16)
 
     def gd_copy():
         return remote(gd_send, gd_recv, gd_s.at[0], gd_r.at[0], device(y, 1 - h, z, l, c))
@@ -453,12 +457,6 @@
     def g_copy(q):
         return remote(gsend.at[q], grecv.at[q], g_s.at[q], g_r.at[q], device(y, 1 - h, z, l, c))
 
-    for n in range(2):
-        w_copy(n).wait_recv()
-    for w in range(2):
-        inward_gu(1, w)
-    for part in chunks:
-        hl_t[1, :, part] = hidden_of(1, part)[4].T.astype(BF16)
     for q in range(4):
         gd_send[:, q * Q : (q + 1) * Q] = dot(hl_t[1], scaled[q]).astype(BF16)[0:FF]
     w_copy(2).wait_recv()
@@ -547,6 +545,19 @@
     relay(2)
     other_grads(1)
     relay(3)
+    other_grads(2)
+
+    for q in range(4):
+        lanes = slice(q * Q, (q + 1) * Q)
+        part = dot(ga_t[0], slots[q, :, 0:Q])
+        o_g[0, :, lanes] = part[0:FF]
+        o_u[0, :, lanes] = part[128 : 128 + FF]
+        o_d[0, :, lanes] = dot(hl_t[0], scaled[q])[0:FF]
+
+    @pl.when(active)
+    def _():
+        p_back[...] = p_own[0:ROWS].astype(F32).T.astype(BF16)
+        p_oth_back[...] = p_oth[...].astype(F32).T.astype(BF16)
 
     def rb_copy(s):
         w, k = s // 4, s % 4
@@ -556,8 +567,14 @@
             down.at[:, pl.ds(pl.multiple_of(r * CAP, CAP), CAP)],
             rb_s.at[s],
             rb_r.at[r],
-            device(y, h, z - k, other(w), h),
+            device(y, h, z - k, l, h),
         )
+
+    def each_column(s, f):
+        if s % 4 == 0:
+            pl.when(idle)(f)
+        else:
+            f()
 
     for n, part in enumerate(chunks):
         for side in range(2):
@@ -566,10 +583,9 @@
             total = dsend[y, side, part].astype(F32) + near[side, part].astype(F32)
             dback[side, part] = (total + chain[side, part].astype(F32)).astype(BF16)
         for i in range(2):
-            each_owner(n * 2 + i, lambda s=n * 2 + i: rb_copy(s).start())
-
-    for q in (2, 3):
-        other_grads(q)
+            each_column(n * 2 + i, lambda s=n * 2 + i: rb_copy(s).start())
+
+    other_grads(3)
 
     def add_down():
         gd_copy().wait_recv()
@@ -591,19 +607,20 @@
             device(y + step, h if hh == 0 else 1 - h, z, l, c),
         )
 
-    def t_copy():
-        return remote(tsend, trecv, t_s.at[0], t_r.at[0], device(y, 1 - h, z, l, c))
-
-    def owner_recv(w, copy):
+    def t_copy(n):
+        target = (device(y, 1 - h, z, l, c), device(y, h, z, 1 - l, c), diagonal)[n]
+        return remote(tsend.at[n], trecv.at[n], t_s.at[n], t_r.at[n], target)
+
+    def recv_all(w, shared, copy):
         for k in range(4):
-            each_peer(k if w == 0 else 4, lambda cc, k=k: copy(w * 8 + k * 2 + cc).wait_recv())
+            each_peer(k if shared else 4, lambda cc, k=k: copy(w * 8 + k * 2 + cc).wait_recv())
 
     @pl.when(active)
     def _():
         po[c] = pb[0]
         for w in range(2):
-            owner_recv(
-                w, lambda r: remote(pb.at[0], po.at[r], pb_s.at[0], pb_r.at[r], device(y, 1 - h, z, l, c))
+            recv_all(
+                w, w == 0, lambda r: remote(pb.at[0], po.at[r], pb_s.at[0], pb_r.at[r], device(y, 1 - h, z, l, c))
             )
         first, second = named_by(meta[0:1], meta[1:2], expert_column(16))
         sums = [jnp.zeros((1, TOK), F32), jnp.zeros((1, TOK), F32)]
@@ -618,12 +635,12 @@
         add_down()
         add_gate_up(0)
         add_gate_up(1)
-        down[:, pl.ds(pl.multiple_of(c * CAP, CAP), CAP)] = dback[:, 0:CAP]
-        sent = jnp.zeros((TOK, 256), F32)
-        kept = jnp.zeros((TOK, 256), F32)
         for w in range(2):
-            owner_recv(
+            into = pl.ds(pl.multiple_of((w * 8 + c) * CAP, CAP), CAP)
+            down[:, into] = dback[:, w * 4 * CAP : w * 4 * CAP + CAP]
+            recv_all(
                 w,
+                True,
                 lambda r: remote(
                     dback.at[:, pl.ds(0, CAP)],
                     down.at[:, pl.ds(r * CAP, CAP)],
@@ -632,21 +649,26 @@
                     device(y, 1 - h, z, l, c),
                 ),
             )
-            rows = slice(w * ROWS, (w + 1) * ROWS)
-            sent += dot(p_back[:, rows], down[1 - h, rows])
-            if w == 1:
-                tsend[...] = sent.astype(BF16)
-                t_copy().start()
-            kept += dot(p_back[:, rows], down[h, rows])
-        o_tok[...] = kept
+            if w == 0:
+                tsend[0] = dot(p_back[...], down[1 - h, 0:ROWS]).astype(BF16)
+                t_copy(0).start()
+                o_tok[...] = dot(p_back[...], down[h, 0:ROWS])
+            else:
+                tsend[1] = dot(p_oth_back[...], down[h, ROWS : 2 * ROWS]).astype(BF16)
+                t_copy(1).start()
+                tsend[2] = dot(p_oth_back[...], down[1 - h, ROWS : 2 * ROWS]).astype(BF16)
+                t_copy(2).start()
+        t_copy(1).wait_recv()
+        o_tok[...] = o_tok[...] + trecv[1].astype(F32)
 
     @pl.when(idle)
     def _():
         add_down()
         add_gate_up(0)
         add_gate_up(1)
-        t_copy().wait_recv()
-        o_tok[...] = trecv[...].astype(F32)
+        t_copy(0).wait_recv()
+        t_copy(2).wait_recv()
+        o_tok[...] = trecv[0].astype(F32) + trecv[2].astype(F32)
         pf_copy(4).wait_recv()
 
     for n in (1, 2, 3):
@@ -660,28 +682,26 @@
     def _():
         each_meta(lambda copy: copy.wait_send())
         for w in range(2):
-            for q in range(2):
+            for q in range(3 - w):
                 for k in range(4):
                     each_peer(k, lambda cc, w=w, k=k, q=q: d_copy(w, k, cc, q).wait_send())
         for n in range(1, 8):
             pf_copy(n).wait_send()
-        t_copy().wait_send()
+        for n in range(3):
+            t_copy(n).wait_send()
 
     for n in range(3):
         w_copy(n).wait_send()
     for k in range(4):
-        for i in range(2):
-            for up in range(2):
-                f_copy(k, i, up).wait_send()
+        for up in range(2):
+            f_copy(k, up, base + 1).wait_send()
+            for i in range(2):
                 e_copy(k, i, up, y).wait_send()
                 v_copy(k, i, up, (y + 1) % 4).wait_send()
     for s in range(8):
 
-        def sent_back(s=s):
-            pb_copy(s).wait_send()
-            rb_copy(s).wait_send()
-
-        each_owner(s, sent_back)
+        each_owner(s, lambda s=s: pb_copy(s).wait_send())
+        each_column(s, lambda s=s: rb_copy(s).wait_send())
     for n in range(4):
         for side in range(2):
             far_copy(n, side).wait_send()
@@ -722,16 +742,17 @@
         scratch_shapes=[
             pltpu.VMEM((8, TOK), F32),
             pltpu.VMEM((8, 8, TOK), F32),
-            pltpu.VMEM((2, TOK, 2 * Q), BF16),
+            pltpu.VMEM((3, TOK, 2 * Q), BF16),
             pltpu.VMEM((TOK, 2 * Q), BF16),
-            pltpu.VMEM((2, ROWS, 2 * Q), BF16),
+            pltpu.VMEM((3, ROWS, 2 * Q), BF16),
             pltpu.VMEM((2, ROWS, Q), BF16),
             pltpu.VMEM((4, ROWS, 2 * Q), BF16),
             pltpu.VMEM((2, 256, D), BF16),
             pltpu.VMEM((2, 128, D), BF16),
             pltpu.VMEM((TOK, TOK), BF16),
             pltpu.VMEM((16 * CAP, TOK), BF16),
-            pltpu.VMEM((TOK, 16 * CAP), BF16),
+            pltpu.VMEM((TOK, ROWS), BF16),
+            pltpu.VMEM((TOK, ROWS), BF16),
             pltpu.VMEM((8 * CAP, TOK), BF16),
             pltpu.VMEM((ROWS, 128), F32),
             pltpu.VMEM((2, ROWS, 256), F32),
@@ -756,19 +777,19 @@
             pltpu.VMEM((FF, D), BF16),
             pltpu.VMEM((4, 2, FF, Q), BF16),
             pltpu.VMEM((4, 2, FF, Q), BF16),
-            pltpu.VMEM((TOK, 256), BF16),
-            pltpu.VMEM((TOK, 256), BF16),
-            dma((7,)),
+            pltpu.VMEM((3, TOK, 256), BF16),
+            pltpu.VMEM((3, TOK, 256), BF16),
+            dma((9,)),
             dma((16,)),
             dma((8,)),
             dma((2,)),
             dma((2,)),
             dma((3,)),
             dma((3,)),
-            dma((32,)),
-            dma((16,)),
-            dma((16,)),
-            dma((16,)),
+            dma((48,)),
+            dma((24,)),
+            dma((8,)),
+            dma((8,)),
             dma((16,)),
             dma((16,)),
             dma((16,)),
@@ -787,8 +808,8 @@
             dma((1,)),
             dma((4,)),
             dma((4,)),
-            dma((1,)),
-            dma((1,)),
+            dma((3,)),
+            dma((3,)),
             dma((8,)),
             dma((4,)),
         ],

time: 88.6 us -> 79.3 us (0.90)
  Pallas kernels: 87.1 us -> 77.8 us
    pallas_call x1, Pallas kernels: 85.6 us -> 76.3 us  [on_device(): pl.pallas_call(kernel, out_shape=(jax.ShapeDtypeStruct((TOK, 256), F32),...]
where the time goes in v3:
time: 79.3 us; the launch traced here: 79.1 us
  Pallas kernels  77.8 us (98%)
    pallas_call x1, Pallas kernels, on_device(): pl.pallas_call(kernel, out_shape=(jax.ShapeDtypeStruct((TOK, 256), F32),...  76.3 us

profile of v3, /device:TPU:1, one launch (start us, length us, event | category | flops | bytes accessed | tf_op | source)
XLA Modules:
  0.0 79.1 jit_solution(11415408009560226632)
XLA Ops:
  0.6 0.0 copy-start
  0.6 0.0 copy-start.1
  0.7 0.7 copy-done
  1.3 0.0 copy-done.1
  1.3 76.3 %expert_backward.1 = (f32[256,256]{1,0:T(8,128)S(1)}, f32[2,256]{1,0:T(2,128)S(1)}, f32[1,96,2048]{2,1,0:T(8,128)S(1)}, f32[1,96,2048]{2,1,0:T(8,128)S(1)}, f32[1,96,2048]{2,1,0:T(8,128)S(1)}) custom-call(bf16[256,2048]{1,0:T(8,128)(2,1)} %tok.1, bf16[256,2048]{1,0:T(8,128)(2,1)} %dy.1, s32[2,256]{1,0:T(2,128)S(1)} %bitcast.3, bf16[2,256]{1,0:T(2,128)(2,1)S(1)} %bitcast.4, ...), custom_call_target="tpu_custom_call" | custom-call | tf_op jit(solution)/shard_map/expert_backward/pallas_call | solution.py:731
  77.6 1.5 %copy_out.1 = (f32[256,256]{1,0:T(8,128)}, f32[2,256]{1,0:T(2,128)}, f32[1,96,2048]{2,1,0:T(8,128)}, f32[1,96,2048]{2,1,0:T(8,128)}, f32[1,96,2048]{2,1,0:T(8,128)}) custom-call(f32[256,256]{1,0:T(8,128)S(1)} %get-tuple-element.15.refs_0_, f32[2,256]{1,0:T(2,128)S(1)} %get-tuple-element.16.refs_1_, f32[1,96,2048]{2,1,0:T(8,128)S(1)} %get-tuple-element.17.refs_2_, ...), custom_call_target="tpu_custom_call" | custom-call | tf_op jit(solution)/shard_map/copy_out/pallas_call | solution.py:829
Async XLA Ops:
  0.6 0.7 copy-start
  0.6 0.7 copy-start.1

commit v4 on v3

--- a/solution.py
+++ b/solution.py
@@ -220,7 +220,7 @@
             raw.at[:, pl.ds(i * Q, Q)],
             raw_s.at[i],
             raw_r.at[i],
-            device(y, h, z, 1 - l, c),
+            device(y, h, z, 1 - l, c) if i == 0 else diagonal,
         )
 
     def meta_copy(w, k, cc):
@@ -326,8 +326,6 @@
         send_out(0, 1, order + (0,))
         for up in range(2):
             f_copy(0, up, base + 1).start()
-        raw_copy(0).wait_send()
-        raw_copy(1).start()
         own_block(0)
         own_block(2)
         meta_copy(1, 0, 0).wait_recv()
@@ -337,7 +335,7 @@
         for r in range(8):
             p_oth[r * CAP : (r + 1) * CAP] = one_hot(where[r : r + 1]).astype(BF16)
         other_block(0)
-        raw_copy(1).wait_send()
+        raw_copy(0).wait_send()
         for n in range(2):
             w_copy(n).start()
         forward(order)
@@ -345,10 +343,12 @@
 
     @pl.when(idle)
     def _():
+        raw_copy(1).start()
         forward((0,))
-        spread(0, (0,))
+        raw_copy(1).wait_send()
         for n in range(2):
             w_copy(n).start()
+        spread(0, (0,))
         forward(order)
         spread(1, (0,))
 
@@ -512,7 +512,8 @@
             csend[side, rows] = total.astype(BF16)
             chain_copy(n, side).start()
 
-    for n, part in enumerate(chunks):
+    def chunk(n):
+        part = chunks[n]
         if n % 2 == 0:
             inward_d(1, n // 2)
         terms = hidden_grads(1, part)[1] + psum[part]
@@ -528,12 +529,12 @@
             dsend[q, 1, part] = low[:, 256:512]
         for side in range(2):
             far_copy(n, side).start()
+        for i in range(2):
+            each_owner(n * 2 + i, lambda s=n * 2 + i: pb_copy(s).start())
+
+    def near_sums(n):
         for side in range(2):
             near_copy(n, side).start()
-        for i in range(2):
-            each_owner(n * 2 + i, lambda s=n * 2 + i: pb_copy(s).start())
-        if n >= 2:
-            relay(n - 2)
 
     def other_grads(q):
         part = dot(ga_t[1], slots[q, :, 0:Q]).astype(BF16)
@@ -541,23 +542,18 @@
         gsend[q, 1] = part[128 : 128 + FF]
         g_copy(q).start()
 
-    other_grads(0)
-    relay(2)
-    other_grads(1)
-    relay(3)
-    other_grads(2)
-
-    for q in range(4):
-        lanes = slice(q * Q, (q + 1) * Q)
-        part = dot(ga_t[0], slots[q, :, 0:Q])
-        o_g[0, :, lanes] = part[0:FF]
-        o_u[0, :, lanes] = part[128 : 128 + FF]
-        o_d[0, :, lanes] = dot(hl_t[0], scaled[q])[0:FF]
-
-    @pl.when(active)
-    def _():
-        p_back[...] = p_own[0:ROWS].astype(F32).T.astype(BF16)
-        p_oth_back[...] = p_oth[...].astype(F32).T.astype(BF16)
+    def own_grads():
+        for q in range(4):
+            lanes = slice(q * Q, (q + 1) * Q)
+            part = dot(ga_t[0], slots[q, :, 0:Q])
+            o_g[0, :, lanes] = part[0:FF]
+            o_u[0, :, lanes] = part[128 : 128 + FF]
+            o_d[0, :, lanes] = dot(hl_t[0], scaled[q])[0:FF]
+
+        @pl.when(active)
+        def _():
+            p_back[...] = p_own[0:ROWS].astype(F32).T.astype(BF16)
+            p_oth_back[...] = p_oth[...].astype(F32).T.astype(BF16)
 
     def rb_copy(s):
         w, k = s // 4, s % 4
@@ -576,7 +572,8 @@
         else:
             f()
 
-    for n, part in enumerate(chunks):
+    def back(n):
+        part = chunks[n]
         for side in range(2):
             near_copy(n, side).wait_recv()
             chain_copy(n, side).wait_recv()
@@ -584,8 +581,6 @@
             dback[side, part] = (total + chain[side, part].astype(F32)).astype(BF16)
         for i in range(2):
             each_column(n * 2 + i, lambda s=n * 2 + i: rb_copy(s).start())
-
-    other_grads(3)
 
     def add_down():
         gd_copy().wait_recv()
@@ -614,6 +609,18 @@
     def recv_all(w, shared, copy):
         for k in range(4):
             each_peer(k if shared else 4, lambda cc, k=k: copy(w * 8 + k * 2 + cc).wait_recv())
+
+    for n in range(4):
+        chunk(n)
+        near_sums(n)
+        if n >= 2:
+            relay(n - 2)
+    other_grads(0)
+    relay(2)
+    other_grads(1)
+    relay(3)
+    other_grads(2)
+    own_grads()
 
     @pl.when(active)
     def _():
@@ -632,9 +639,13 @@
         pf[0] = jnp.concatenate(sums + [jnp.zeros((6, TOK), F32)], axis=0)
         for n in range(1, 8):
             pf_copy(n).start()
-        add_down()
-        add_gate_up(0)
-        add_gate_up(1)
+
+    for n in range(4):
+        back(n)
+    other_grads(3)
+
+    @pl.when(active)
+    def _():
         for w in range(2):
             into = pl.ds(pl.multiple_of((w * 8 + c) * CAP, CAP), CAP)
             down[:, into] = dback[:, w * 4 * CAP : w * 4 * CAP + CAP]
@@ -658,6 +669,9 @@
                 t_copy(1).start()
                 tsend[2] = dot(p_oth_back[...], down[1 - h, ROWS : 2 * ROWS]).astype(BF16)
                 t_copy(2).start()
+        add_down()
+        add_gate_up(0)
+        add_gate_up(1)
         t_copy(1).wait_recv()
         o_tok[...] = o_tok[...] + trecv[1].astype(F32)
 

time: 79.3 us -> 76.8 us (0.968)
  Pallas kernels: 77.8 us -> 74.6 us
    pallas_call x1, Pallas kernels: 76.3 us -> 73 us  [on_device(): pl.pallas_call(kernel, out_shape=(jax.ShapeDtypeStruct((TOK, 256), F32),...]
where the time goes in v4:
time: 76.8 us; the launch traced here: 75.9 us
  Pallas kernels  74.6 us (97%)
    pallas_call x1, Pallas kernels, on_device(): pl.pallas_call(kernel, out_shape=(jax.ShapeDtypeStruct((TOK, 256), F32),...  73 us

profile of v4, /device:TPU:1, one launch (start us, length us, event | category | flops | bytes accessed | tf_op | source)
XLA Modules:
  0.0 75.9 jit_solution(9052290729151979271)
XLA Ops:
  0.6 0.0 copy-start
  0.6 0.0 copy-start.1
  0.7 0.7 copy-done
  1.3 0.0 copy-done.1
  1.3 73.0 %expert_backward.1 = (f32[256,256]{1,0:T(8,128)S(1)}, f32[2,256]{1,0:T(2,128)S(1)}, f32[1,96,2048]{2,1,0:T(8,128)S(1)}, f32[1,96,2048]{2,1,0:T(8,128)S(1)}, f32[1,96,2048]{2,1,0:T(8,128)S(1)}) custom-call(bf16[256,2048]{1,0:T(8,128)(2,1)} %tok.1, bf16[256,2048]{1,0:T(8,128)(2,1)} %dy.1, s32[2,256]{1,0:T(2,128)S(1)} %bitcast.3, bf16[2,256]{1,0:T(2,128)(2,1)S(1)} %bitcast.4, ...), custom_call_target="tpu_custom_call" | custom-call | tf_op jit(solution)/shard_map/expert_backward/pallas_call | solution.py:745
  74.4 1.5 %copy_out.1 = (f32[256,256]{1,0:T(8,128)}, f32[2,256]{1,0:T(2,128)}, f32[1,96,2048]{2,1,0:T(8,128)}, f32[1,96,2048]{2,1,0:T(8,128)}, f32[1,96,2048]{2,1,0:T(8,128)}) custom-call(f32[256,256]{1,0:T(8,128)S(1)} %get-tuple-element.15.refs_0_, f32[2,256]{1,0:T(2,128)S(1)} %get-tuple-element.16.refs_1_, f32[1,96,2048]{2,1,0:T(8,128)S(1)} %get-tuple-element.17.refs_2_, ...), custom_call_target="tpu_custom_call" | custom-call | tf_op jit(solution)/shard_map/copy_out/pallas_call | solution.py:843
Async XLA Ops:
  0.6 0.7 copy-start
  0.6 0.7 copy-start.1

commit v5 on v4

--- a/solution.py
+++ b/solution.py
@@ -335,19 +335,19 @@
         for r in range(8):
             p_oth[r * CAP : (r + 1) * CAP] = one_hot(where[r : r + 1]).astype(BF16)
         other_block(0)
+        other_block(1)
         raw_copy(0).wait_send()
         for n in range(2):
             w_copy(n).start()
         forward(order)
-        other_block(1)
 
     @pl.when(idle)
     def _():
         raw_copy(1).start()
-        forward((0,))
         raw_copy(1).wait_send()
         for n in range(2):
             w_copy(n).start()
+        forward((0,))
         spread(0, (0,))
         forward(order)
         spread(1, (0,))

time: 76.8 us -> 76.6 us (level)
  no operation moved by 1% of the time
where the time goes in v5:
time: 76.6 us; the launch traced here: 75.4 us
  Pallas kernels  74.1 us (97%)
    pallas_call x1, Pallas kernels, on_device(): pl.pallas_call(kernel, out_shape=(jax.ShapeDtypeStruct((TOK, 256), F32),...  72.6 us
    pallas_call x1, Pallas kernels, on_device(): pl.pallas_call(copy_out, out_shape=tuple((jax.ShapeDtypeStruct(v.shape, v...  1.53 us

profile of v5, /device:TPU:1, one launch (start us, length us, event | category | flops | bytes accessed | tf_op | source)
XLA Modules:
  0.0 75.4 jit_solution(16542847543331259611)
XLA Ops:
  0.6 0.0 copy-start
  0.6 0.0 copy-start.1
  0.7 0.7 copy-done
  1.3 0.0 copy-done.1
  1.3 72.6 %expert_backward.1 = (f32[256,256]{1,0:T(8,128)S(1)}, f32[2,256]{1,0:T(2,128)S(1)}, f32[1,96,2048]{2,1,0:T(8,128)S(1)}, f32[1,96,2048]{2,1,0:T(8,128)S(1)}, f32[1,96,2048]{2,1,0:T(8,128)S(1)}) custom-call(bf16[256,2048]{1,0:T(8,128)(2,1)} %tok.1, bf16[256,2048]{1,0:T(8,128)(2,1)} %dy.1, s32[2,256]{1,0:T(2,128)S(1)} %bitcast.3, bf16[2,256]{1,0:T(2,128)(2,1)S(1)} %bitcast.4, ...), custom_call_target="tpu_custom_call" | custom-call | tf_op jit(solution)/shard_map/expert_backward/pallas_call | solution.py:745
  73.9 1.5 %copy_out.1 = (f32[256,256]{1,0:T(8,128)}, f32[2,256]{1,0:T(2,128)}, f32[1,96,2048]{2,1,0:T(8,128)}, f32[1,96,2048]{2,1,0:T(8,128)}, f32[1,96,2048]{2,1,0:T(8,128)}) custom-call(f32[256,256]{1,0:T(8,128)S(1)} %get-tuple-element.15.refs_0_, f32[2,256]{1,0:T(2,128)S(1)} %get-tuple-element.16.refs_1_, f32[1,96,2048]{2,1,0:T(8,128)S(1)} %get-tuple-element.17.refs_2_, ...), custom_call_target="tpu_custom_call" | custom-call | tf_op jit(solution)/shard_map/copy_out/pallas_call | solution.py:843
Async XLA Ops:
  0.6 0.7 copy-start
  0.6 0.7 copy-start.1
